TPU v7x, 128 devices: a whole 4x4x4 slice. The times are simulated.
128 devices in a mesh: row: 16 (over y_hi, x, core), col: 8 (over z, y_lo).
Axes of the slice: x: 4, y: 4 (y_hi: 2, y_lo: 2; y = y_hi * 2 + y_lo), z: 4, core: 2. Of those that a mesh axis runs over, the one named last changes fastest.
Arguments:
- cycle_inter: float32 [1536, 1536, 128], P(None, ('row', 'col')), may hold values from -6 to 6
- integrals: float32 [1536, 1536, 128], P(None, ('row', 'col')), may hold values from -0.005859375 to 0.005859375
Outputs:
- ladder: float32 [128, 128], P('row')
All inputs are finite; a program needn't handle non-finite values.
Results may differ from a plain program's by a relative error of at most 0.0003.
Values sent between devices are 32-bit elements; how exact they have to be, the bound alone decides.
No kernel may reach another device: no remote copies, remote signals or barrier semaphores. Data moves between devices by JAX's collectives and lax.ppermute only.
A program may use at most 128 MiB of HBM per device.

v0:
```python
import jax
import jax.numpy as jnp
from jax import lax
from jax.sharding import PartitionSpec as P


def body(cycle_inter, integrals):
    row_count = lax.axis_size("row")
    col_count = lax.axis_size("col")
    local_width = cycle_inter.shape[1]
    occupied = cycle_inter.shape[2]
    slab_pairs = integrals.shape[2]
    received = lax.all_to_all(cycle_inter, ("row", "col"), split_axis=0, concat_axis=1, tiled=True)
    amplitudes = cycle_inter - jnp.swapaxes(received, 0, 1)
    device_rank = lax.axis_index("row") * col_count + lax.axis_index("col")
    first_column = device_rank * local_width
    column_ids = first_column + jnp.arange(local_width, dtype=jnp.int32)
    block_rows = 128
    needed_blocks = (first_column + local_width + block_rows - 1) // block_rows

    def accumulate(block_index, summed):
        offset = block_index * block_rows
        amp_block = lax.dynamic_slice_in_dim(amplitudes, offset, block_rows, 0)
        integral_block = lax.dynamic_slice_in_dim(integrals, offset, block_rows, 0)
        row_ids = offset + jnp.arange(block_rows, dtype=jnp.int32)
        upper_mask = (row_ids[:, None] < column_ids[None, :]).astype(jnp.float32)
        amp_block = amp_block * upper_mask[:, :, None]
        return summed + jnp.einsum(
            "cdi,cda->ia", amp_block, integral_block, precision=lax.Precision.HIGHEST
        )

    partial_sum = lax.fori_loop(
        0, needed_blocks, accumulate, jnp.zeros((occupied, slab_pairs), jnp.float32)
    )
    owned_rows = occupied // row_count
    summed = lax.psum(partial_sum, ("row", "col"))
    return lax.dynamic_slice_in_dim(summed, lax.axis_index("row") * owned_rows, owned_rows, 0)


def solution(mesh):
    return jax.shard_map(
        body,
        mesh=mesh,
        in_specs=(P(None, ("row", "col"), None), P(None, ("row", "col"), None)),
        out_specs=P("row", None),
        check_vma=False,
    )
```

profile of v0, /device:TPU:0, one launch (start us, length us, event | category | flops | bytes accessed | tf_op | source)
XLA Modules:
  0.0 408.9 jit_solution(1875631772332710024)
XLA Ops:
  6.5 12.7 %copy.7 = f32[1536,12,128]{2,1,0:T(8,128)} copy(f32[1536,12,128]{2,0,1:T(8,128)} %param.4) | data formatting | bytes 18874368 | tf_op args[0]
  19.2 11.6 %all-to-all-start = ((f32[1536,12,128]{2,1,0:T(8,128)}), f32[1536,12,128]{2,1,0:T(8,128)}, u32[]{:S(2)}, u32[]{:S(2)}) async-start(f32[1536,12,128]{2,1,0:T(8,128)} %copy.7), calls=%async_computation | async-start | bytes 25165824 | tf_op jit(solution)/shard_map/all_to_all | solution.py:13
  30.8 0.0 all-reduce.2.cloned.1.call-start
  30.9 162.3 %all-to-all-done = f32[1536,12,128]{2,1,0:T(8,128)} async-done(((f32[1536,12,128]{2,1,0:T(8,128)}), f32[1536,12,128]{2,1,0:T(8,128)}, u32[]{:S(2)}, u32[]{:S(2)}) %all-to-all-start) | async-done | bytes 9437216 | tf_op jit(solution)/shard_map/all_to_all | solution.py:13
  193.1 10.3 %copy.9 = f32[12,128,12,128]{3,2,1,0:T(8,128)} copy(f32[12,128,12,128]{3,2,0,1:T(8,128)} %bitcast.2) | data formatting | bytes 18874368 | tf_op jit(solution)/shard_map/all_to_all | solution.py:13
  203.5 12.0 %all_to_all.16 = f32[12,1536,128]{2,1,0:T(8,128)} reshape(f32[12,128,12,128]{3,2,1,0:T(8,128)} %copy.9) | data formatting | bytes 18874368 | tf_op jit(solution)/shard_map/all_to_all | solution.py:13
  215.4 10.9 %bitcast_subtract_fusion = f32[1536,12,128]{2,0,1:T(8,128)} fusion(f32[1536,12,128]{2,0,1:T(8,128)} %param.4, f32[12,1536,128]{2,1,0:T(8,128)} %all_to_all.16), kind=kLoop, calls=%fused_computation.11 | loop fusion | flops 2359296 | bytes 28311552 | tf_op jit(solution)/shard_map/sub | solution.py:14
  226.4 3.6 while.11
  226.4 1.2 constant_dynamic-slice_fusion.3
  227.6 0.3 copy.15
  227.9 0.1 compare_convert_fusion.2
  227.9 2.1 fusion.12
  230.0 0.0 copy-start
  230.0 0.6 copy-done
  230.7 0.0 all-reduce.2.cloned.1.call-update
  230.7 170.2 %all-reduce.2.cloned.1.call-done = f32[128,128]{1,0:T(8,128)} async-done(((f32[128,128]{1,0:T(8,128)}), f32[128,128]{1,0:T(8,128)}) %all-reduce.2.cloned.1.call-update) | async-done | bytes 65552 | tf_op jit(solution)/shard_map/psum | solution.py:36
  400.8 1.3 constant_dynamic-slice_fusion.1
  (3 shorter events, 0.0 us)
Async XLA Ops:
  19.2 173.9 %all-to-all-start = ((f32[1536,12,128]{2,1,0:T(8,128)}), f32[1536,12,128]{2,1,0:T(8,128)}, u32[]{:S(2)}, u32[]{:S(2)}) async-start(f32[1536,12,128]{2,1,0:T(8,128)} %copy.7), calls=%async_computation | async-start | bytes 25165824 | tf_op jit(solution)/shard_map/all_to_all | solution.py:13
  30.8 370.0 %all-reduce.2.cloned.1.call-start = ((), (), s32[]{:S(2)}) async-start(), calls=%async_computation.1 | async-start | bytes 131072 | tf_op jit(solution)/shard_map/psum | solution.py:36
  230.0 0.6 copy-start
Sparse Core Ops, SparseCore 0:
  230.8 169.9 all-reduce.1
where the time goes:
time: 414 us; the launch traced here: 409 us
  waiting for transfers between devices  332 us (80%)
  local copies, waits for them, and re-layouts  38.3 us (9%)
  between operations  13.4 us (3%)
  starting transfers between devices  11.7 us (3%)
  other arithmetic  11 us (3%)
    psum x1, waiting for transfers between devices, body(): summed = lax.psum(partial_sum, ('row', 'col'))  170 us
    all_to_all x1, waiting for transfers between devices, body(): lax.all_to_all(cycle_inter, ('row', 'col'), split_axis=0, concat_axis=1,...  162 us
    all_to_all x2, local copies, waits for them, and re-layouts, body(): lax.all_to_all(cycle_inter, ('row', 'col'), split_axis=0, concat_axis=1,...  22.3 us
    unnamed x3, local copies, waits for them, and re-layouts  13.3 us
    all_to_all x1, starting transfers between devices, body(): lax.all_to_all(cycle_inter, ('row', 'col'), split_axis=0, concat_axis=1,...  11.6 us
    sub x1, other arithmetic, body(): amplitudes = cycle_inter - jnp.swapaxes(received, 0, 1)  10.9 us
  transfers between devices with their start and end apart: 2, of which 2 were waited for; matrix products, arithmetic and copies ran while one was open for 0% of the time, Pallas kernels for 0%

commit v1 on v0

v1 whole, which is shorter than its diff:
```python
import functools

import jax
import jax.numpy as jnp
from jax import lax
from jax.experimental import pallas as pl
from jax.experimental.pallas import tpu as pltpu
from jax.sharding import PartitionSpec as P

AXES = ("row", "col")
DEVICES = 128
WIDTH = 12
HALF = WIDTH // 2
BLOCK = WIDTH * HALF
LANES = 128
PEERS = 16
GROUPS = DEVICES // PEERS
ROWS = PEERS * WIDTH
TERMS = PEERS * BLOCK
ROW_DEVICES = 16
COL_DEVICES = 8
OUT_ROWS = LANES // ROW_DEVICES
VMEM_LIMIT = 56 * 1024 * 1024


def split(value):
    high = value.astype(jnp.bfloat16)
    low = (value - high.astype(jnp.float32)).astype(jnp.bfloat16)
    return high, low


def dot(a, b):
    return lax.dot_general(a, b, (((1,), (0,)), ((), ())), preferred_element_type=jnp.float32)


def fold(acc):
    top = acc[:LANES, :LANES] + acc[:LANES, LANES:]
    return top + (acc[LANES:, :LANES] + acc[LANES:, LANES:])


def pack_kernel(rank_ref, x_ref, v_ref, out_ref):
    rank = rank_ref[0]
    group = pl.program_id(0)
    for i in range(PEERS):
        peer = group * PEERS + i

        @pl.when(peer > rank)
        def _():
            for c in range(HALF):
                out_ref[i, pl.ds(WIDTH * c, WIDTH), :] = x_ref[c, pl.ds(WIDTH * i, WIDTH), :]

        @pl.when(peer < rank)
        def _():
            for d in range(WIDTH):
                out_ref[i, pl.ds(HALF * d, HALF), :] = v_ref[d, pl.ds(WIDTH * i + HALF, HALF), :]

        @pl.when(peer == rank)
        def _():
            out_ref[i] = jnp.zeros((BLOCK, LANES), jnp.float32)


def pack(rank, x, v):
    return pl.pallas_call(
        pack_kernel,
        grid_spec=pltpu.PrefetchScalarGridSpec(
            num_scalar_prefetch=1,
            grid=(GROUPS,),
            in_specs=[
                pl.BlockSpec((HALF, ROWS, LANES), lambda g, r: (0, jnp.maximum(g, r[0] // PEERS), 0)),
                pl.BlockSpec((WIDTH, ROWS, LANES), lambda g, r: (0, jnp.minimum(g, r[0] // PEERS), 0)),
            ],
            out_specs=pl.BlockSpec((PEERS, BLOCK, LANES), lambda g, r: (g, 0, 0)),
        ),
        out_shape=jax.ShapeDtypeStruct((DEVICES, BLOCK, LANES), jnp.float32),
        compiler_params=pltpu.CompilerParams(vmem_limit_bytes=VMEM_LIMIT),
        cost_estimate=pl.CostEstimate(flops=0, bytes_accessed=12_000_000, transcendentals=0),
        name="pack",
    )(rank, x, v)


def local_kernel(rank_ref, x_ref, v_ref, left_ref, direct_ref, terms_ref, own_x_ref, own_v_ref, acc_ref):
    rank = rank_ref[0]
    group = pl.program_id(0)
    own_group = rank // PEERS

    @pl.when(group == 0)
    def _():
        acc_ref[...] = jnp.zeros_like(acc_ref)

    for i in range(PEERS):
        peer = group * PEERS + i

        @pl.when(peer > rank)
        def _():
            for c in range(HALF):
                terms_ref[pl.ds(BLOCK * i + c, WIDTH, stride=HALF), :] = x_ref[HALF + c, pl.ds(WIDTH * i, WIDTH), :]

        @pl.when(peer < rank)
        def _():
            for d in range(WIDTH):
                terms_ref[pl.ds(BLOCK * i + d, HALF, stride=WIDTH), :] = v_ref[d, pl.ds(WIDTH * i, HALF), :]

        @pl.when(peer == rank)
        def _():
            terms_ref[pl.ds(BLOCK * i, BLOCK), :] = jnp.zeros((BLOCK, LANES), jnp.float32)
            for c in range(WIDTH):
                own_x_ref[pl.ds(WIDTH * c, WIDTH), :] = x_ref[c, pl.ds(WIDTH * i, WIDTH), :]
                own_v_ref[pl.ds(c, WIDTH, stride=WIDTH), :] = v_ref[c, pl.ds(WIDTH * i, WIDTH), :]

    high, low = split(terms_ref[...].T)
    left_ref[0, :LANES, :] = high
    left_ref[0, LANES:, :] = low

    def add(x_rows, v_rows):
        left = jnp.concatenate(split(x_rows.T), axis=0)
        right = jnp.concatenate(split(v_rows), axis=1)
        acc_ref[...] += dot(left, right)

    @pl.when(group < own_group)
    def _():
        for d in range(WIDTH):
            add(x_ref[d], v_ref[d])

    @pl.when(group == own_group)
    def _():
        ids = group * ROWS + lax.broadcasted_iota(jnp.int32, (ROWS, LANES), 0)
        for d in range(WIDTH):
            add(x_ref[d], jnp.where(ids < rank * WIDTH + d, v_ref[d], 0.0))
        pair = lax.broadcasted_iota(jnp.int32, (WIDTH * WIDTH, LANES), 0)
        upper = pair % WIDTH > pair // WIDTH
        add(own_x_ref[...], jnp.where(upper, -own_v_ref[...], 0.0))

    @pl.when(group == GROUPS - 1)
    def _():
        direct_ref[...] = fold(acc_ref[...])


def local(rank, x, v):
    return pl.pallas_call(
        local_kernel,
        grid_spec=pltpu.PrefetchScalarGridSpec(
            num_scalar_prefetch=1,
            grid=(GROUPS,),
            in_specs=[
                pl.BlockSpec((WIDTH, ROWS, LANES), lambda g, r: (0, g, 0)),
                pl.BlockSpec((WIDTH, ROWS, LANES), lambda g, r: (0, jnp.minimum(g, r[0] // PEERS), 0)),
            ],
            out_specs=[
                pl.BlockSpec((1, 2 * LANES, TERMS), lambda g, r: (g, 0, 0)),
                pl.BlockSpec((LANES, LANES), lambda g, r: (0, 0)),
            ],
            scratch_shapes=[
                pltpu.VMEM((TERMS, LANES), jnp.float32),
                pltpu.VMEM((WIDTH * WIDTH, LANES), jnp.float32),
                pltpu.VMEM((WIDTH * WIDTH, LANES), jnp.float32),
                pltpu.VMEM((2 * LANES, 2 * LANES), jnp.float32),
            ],
        ),
        out_shape=[
            jax.ShapeDtypeStruct((GROUPS, 2 * LANES, TERMS), jnp.bfloat16),
            jax.ShapeDtypeStruct((LANES, LANES), jnp.float32),
        ],
        compiler_params=pltpu.CompilerParams(vmem_limit_bytes=VMEM_LIMIT),
        cost_estimate=pl.CostEstimate(flops=20_000_000_000, bytes_accessed=30_000_000, transcendentals=0),
        name="local",
    )(rank, x, v)


def mirror_kernel(rank_ref, left_ref, received_ref, direct_ref, out_ref, below_ref, above_ref):
    rank = rank_ref[0]
    group = pl.program_id(0)
    own_group = rank // PEERS

    @pl.when(group == 0)
    def _():
        below_ref[...] = jnp.zeros_like(below_ref)
        above_ref[...] = jnp.zeros_like(above_ref)

    def product(received):
        right = jnp.concatenate(split(received), axis=1)
        return dot(left_ref[0], right)

    received = received_ref[...].reshape(TERMS, LANES)

    @pl.when(group < own_group)
    def _():
        below_ref[...] += product(received)

    @pl.when(group > own_group)
    def _():
        above_ref[...] += product(received)

    @pl.when(group == own_group)
    def _():
        term = lax.broadcasted_iota(jnp.int32, (TERMS, LANES), 0)
        first = (rank - group * PEERS) * BLOCK
        below_ref[...] += product(jnp.where(term < first, received, 0.0))
        above_ref[...] += product(jnp.where(term >= first + BLOCK, received, 0.0))

    @pl.when(group == GROUPS - 1)
    def _():
        total = direct_ref[...] - (fold(above_ref[...]) + fold(below_ref[...]).T)
        for row in range(ROW_DEVICES):
            rows = total[OUT_ROWS * row : OUT_ROWS * (row + 1), :]
            for col in range(COL_DEVICES):
                out_ref[COL_DEVICES * row + col] = rows


def mirror(rank, left, received, direct):
    return pl.pallas_call(
        mirror_kernel,
        grid_spec=pltpu.PrefetchScalarGridSpec(
            num_scalar_prefetch=1,
            grid=(GROUPS,),
            in_specs=[
                pl.BlockSpec((1, 2 * LANES, TERMS), lambda g, r: (g, 0, 0)),
                pl.BlockSpec((PEERS, BLOCK, LANES), lambda g, r: (g, 0, 0)),
                pl.BlockSpec((LANES, LANES), lambda g, r: (0, 0)),
            ],
            out_specs=pl.BlockSpec((DEVICES, OUT_ROWS, LANES), lambda g, r: (0, 0, 0)),
            scratch_shapes=[
                pltpu.VMEM((2 * LANES, 2 * LANES), jnp.float32),
                pltpu.VMEM((2 * LANES, 2 * LANES), jnp.float32),
            ],
        ),
        out_shape=jax.ShapeDtypeStruct((DEVICES, OUT_ROWS, LANES), jnp.float32),
        compiler_params=pltpu.CompilerParams(vmem_limit_bytes=VMEM_LIMIT),
        cost_estimate=pl.CostEstimate(flops=2_500_000_000, bytes_accessed=10_000_000, transcendentals=0),
        name="mirror",
    )(rank, left, received, direct)


def body(cycle_inter, integrals):
    x = jnp.swapaxes(cycle_inter, 0, 1)
    v = jnp.swapaxes(integrals, 0, 1)
    rank = (lax.axis_index("row") * lax.axis_size("col") + lax.axis_index("col")).astype(jnp.int32).reshape(1)
    received = lax.all_to_all(pack(rank, x, v), AXES, 0, 0, tiled=True)
    left, direct = local(rank, x, v)
    parts = lax.all_to_all(mirror(rank, left, received, direct), AXES, 0, 0, tiled=True)
    return jnp.sum(parts, axis=0)


def solution(mesh):
    return jax.shard_map(
        body,
        mesh=mesh,
        in_specs=(P(None, AXES, None), P(None, AXES, None)),
        out_specs=P("row", None),
        check_vma=False,
    )
```

time: 414 us -> 108 us (0.26)
  waiting for transfers between devices: 332 us -> 47.2 us
  local copies, waits for them, and re-layouts: 38.3 us -> 0 us
  Pallas kernels: 0 us -> 26.9 us
  blocking collectives: 0 us -> 19.5 us
  between operations: 13.4 us -> 0.01 us
  other arithmetic: 11 us -> 0.73 us
    psum x1 -> x0, waiting for transfers between devices: 170 us -> none  [body(): summed = lax.psum(partial_sum, ('row', 'col'))]
    all_to_all x1, waiting for transfers between devices: 162 us -> 47.2 us  [body(): received = lax.all_to_all(pack(rank, x, v), AXES, 0, 0, tiled=True)]
    pallas_call x0 -> x3, Pallas kernels: none -> 26.9 us  [the longest x1 10.6 us: local(): pl.pallas_call(local_kernel, grid_spec=pltpu.PrefetchScalarGridSpec(num_s...]
    all_to_all x2 -> x0, local copies, waits for them, and re-layouts: 22.3 us -> none  [body(): lax.all_to_all(cycle_inter, ('row', 'col'), split_axis=0, concat_axis=1,...]
    all_to_all x0 -> x1, blocking collectives: none -> 19.5 us  [body(): lax.all_to_all(mirror(rank, left, received, direct), AXES, 0, 0, tiled=True)]
    unnamed x3 -> x0, local copies, waits for them, and re-layouts: 13.3 us -> none
    sub x1 -> x0, other arithmetic: 10.9 us -> none  [body(): amplitudes = cycle_inter - jnp.swapaxes(received, 0, 1)]
  transfers between devices with their start and end apart: 2 -> 1, of which waited for: 2 -> 1; matrix products, arithmetic and copies ran while one was open for 0% -> 0% of each run, Pallas kernels for 0% -> 10%
where the time goes in v1:
time: 108 us; the launch traced here: 107 us
  waiting for transfers between devices  47.2 us (44%)
  Pallas kernels  26.9 us (25%)
  blocking collectives  19.5 us (18%)
  starting transfers between devices  12.5 us (12%)
    all_to_all x1, waiting for transfers between devices, body(): received = lax.all_to_all(pack(rank, x, v), AXES, 0, 0, tiled=True)  47.2 us
    all_to_all x1, blocking collectives, body(): lax.all_to_all(mirror(rank, left, received, direct), AXES, 0, 0, tiled=True)  19.5 us
    all_to_all x1, starting transfers between devices, body(): received = lax.all_to_all(pack(rank, x, v), AXES, 0, 0, tiled=True)  12.5 us
    pallas_call x1, Pallas kernels, local(): pl.pallas_call(local_kernel, grid_spec=pltpu.PrefetchScalarGridSpec(num_s...  10.6 us
    pallas_call x1, Pallas kernels, mirror(): pl.pallas_call(mirror_kernel, grid_spec=pltpu.PrefetchScalarGridSpec(num_...  8.41 us
    pallas_call x1, Pallas kernels, pack(): pl.pallas_call(pack_kernel, grid_spec=pltpu.PrefetchScalarGridSpec(num_sc...  7.88 us
  transfers between devices with their start and end apart: 1, of which 1 were waited for; matrix products, arithmetic and copies ran while one was open for 0% of the time, Pallas kernels for 10%

profile of v1, /device:TPU:0, one launch (start us, length us, event | category | flops | bytes accessed | tf_op | source)
XLA Modules:
  0.0 106.9 jit_solution(15811037645512119644)
XLA Ops:
  0.0 7.9 %pack.1 = f32[128,72,128]{2,1,0:T(8,128)} custom-call(s32[1]{0:T(128)} %bitcast.rank_ref, f32[12,1536,128]{2,1,0:T(8,128)} %bitcast.3, f32[12,1536,128]{2,1,0:T(8,128)} %bitcast.5), custom_call_target="tpu_custom_call" | custom-call | bytes 12000000 | tf_op jit(solution)/shard_map/pack/pallas_call | solution.py:63
  7.9 12.5 %all-to-all-start = ((f32[128,72,128]{2,1,0:T(8,128)}), f32[128,72,128]{2,1,0:T(8,128)}, u32[]{:S(2)}, u32[]{:S(2)}) async-start(f32[128,72,128]{2,1,0:T(8,128)} %pack.1), calls=%async_computation | async-start | bytes 9437184 | tf_op jit(solution)/shard_map/all_to_all | solution.py:237
  20.4 10.6 %local.1 = (bf16[8,256,1152]{2,1,0:T(8,128)(2,1)}, f32[128,128]{1,0:T(8,128)}) custom-call(s32[1]{0:T(128)} %bitcast.rank_ref, f32[12,1536,128]{2,1,0:T(8,128)} %bitcast.4, f32[12,1536,128]{2,1,0:T(8,128)} %bitcast.6), custom_call_target="tpu_custom_call" | custom-call | flops 20000000000 | bytes 30000000 | tf_op jit(solution)/shard_map/local/pallas_call | solution.py:139
  31.0 47.2 %all-to-all-done.received_ref = f32[128,72,128]{2,1,0:T(8,128)} async-done(((f32[128,72,128]{2,1,0:T(8,128)}), f32[128,72,128]{2,1,0:T(8,128)}, u32[]{:S(2)}, u32[]{:S(2)}) %all-to-all-start) | async-done | bytes 4718624 | tf_op jit(solution)/shard_map/all_to_all | solution.py:237
  78.2 8.4 %mirror.1 = f32[128,8,128]{2,1,0:T(8,128)} custom-call(s32[1]{0:T(128)} %bitcast.rank_ref, bf16[8,256,1152]{2,1,0:T(8,128)(2,1)} %get-tuple-element.7.left_ref, f32[128,72,128]{2,1,0:T(8,128)} %all-to-all-done.received_ref, f32[128,128]{1,0:T(8,128)} %get-tuple-element.8.direct_ref), custom_call_target="tpu_custom_call" | custom-call | flops 2500000000 | bytes 10000000 | tf_op jit(solution)/shard_map/mirror/pallas_call | solution.py:210
  86.6 19.5 %all_to_all.10 = f32[128,8,128]{2,1,0:T(8,128)S(1)} all-to-all(f32[128,8,128]{2,1,0:T(8,128)} %mirror.1), channel_id=1, replica_groups=mesh['row'=16,'col'=8] {'row','col'}, dimensions={0} | all-to-all | bytes 1048576 | tf_op jit(solution)/shard_map/all_to_all | solution.py:239
  106.1 0.7 reduce_sum.9
Async XLA Ops:
  7.9 70.3 %all-to-all-start = ((f32[128,72,128]{2,1,0:T(8,128)}), f32[128,72,128]{2,1,0:T(8,128)}, u32[]{:S(2)}, u32[]{:S(2)}) async-start(f32[128,72,128]{2,1,0:T(8,128)} %pack.1), calls=%async_computation | async-start | bytes 9437184 | tf_op jit(solution)/shard_map/all_to_all | solution.py:237

commit v2 on v1

--- a/solution.py
+++ b/solution.py
@@ -1,5 +1,3 @@
-import functools
-
 import jax
 import jax.numpy as jnp
 from jax import lax
@@ -13,7 +11,10 @@
 HALF = WIDTH // 2
 BLOCK = WIDTH * HALF
 LANES = 128
-PEERS = 16
+PACK_PEERS = 16
+PACK_GROUPS = DEVICES // PACK_PEERS
+PACK_ROWS = PACK_PEERS * WIDTH
+PEERS = 32
 GROUPS = DEVICES // PEERS
 ROWS = PEERS * WIDTH
 TERMS = PEERS * BLOCK
@@ -38,40 +39,96 @@
     return top + (acc[LANES:, :LANES] + acc[LANES:, LANES:])
 
 
-def pack_kernel(rank_ref, x_ref, v_ref, out_ref):
+def pack_kernel(rank_ref, x_ref, v_ref, out_ref, x_rows, v_rows, packed, x_sem, v_sem, out_sem):
     rank = rank_ref[0]
-    group = pl.program_id(0)
-    for i in range(PEERS):
-        peer = group * PEERS + i
-
-        @pl.when(peer > rank)
-        def _():
-            for c in range(HALF):
-                out_ref[i, pl.ds(WIDTH * c, WIDTH), :] = x_ref[c, pl.ds(WIDTH * i, WIDTH), :]
-
-        @pl.when(peer < rank)
-        def _():
-            for d in range(WIDTH):
-                out_ref[i, pl.ds(HALF * d, HALF), :] = v_ref[d, pl.ds(WIDTH * i + HALF, HALF), :]
-
-        @pl.when(peer == rank)
-        def _():
-            out_ref[i] = jnp.zeros((BLOCK, LANES), jnp.float32)
+    own_group = rank // PACK_PEERS
+
+    def x_copy(group):
+        rows = pl.ds(group * PACK_ROWS, PACK_ROWS)
+        return pltpu.make_async_copy(x_ref.at[pl.ds(0, HALF), rows], x_rows.at[group], x_sem.at[group])
+
+    def v_copy(group):
+        rows = pl.ds(group * PACK_ROWS, PACK_ROWS)
+        return pltpu.make_async_copy(v_ref.at[:, rows], v_rows.at[group], v_sem.at[group])
+
+    def pack_x(group, i):
+        for c in range(HALF):
+            rows = x_rows[group, c, pl.ds(WIDTH * i, WIDTH), :]
+            packed[group * PACK_PEERS + i, pl.ds(WIDTH * c, WIDTH), :] = rows
+
+    def pack_v(group, i):
+        for d in range(WIDTH):
+            rows = v_rows[group, d, pl.ds(WIDTH * i + HALF, HALF), :]
+            packed[group * PACK_PEERS + i, pl.ds(HALF * d, HALF), :] = rows
+
+    for group in range(PACK_GROUPS):
+
+        @pl.when(group >= own_group)
+        def _():
+            x_copy(group).start()
+
+        @pl.when(group <= own_group)
+        def _():
+            v_copy(group).start()
+
+    def step(group, _):
+        @pl.when(group >= own_group)
+        def _():
+            x_copy(group).wait()
+
+        @pl.when(group <= own_group)
+        def _():
+            v_copy(group).wait()
+
+        @pl.when(group > own_group)
+        def _():
+            for i in range(PACK_PEERS):
+                pack_x(group, i)
+
+        @pl.when(group < own_group)
+        def _():
+            for i in range(PACK_PEERS):
+                pack_v(group, i)
+
+        @pl.when(group == own_group)
+        def _():
+            for i in range(PACK_PEERS):
+                below = group * PACK_PEERS + i < rank
+
+                @pl.when(below)
+                def _():
+                    pack_v(group, i)
+
+                @pl.when(jnp.logical_not(below))
+                def _():
+                    pack_x(group, i)
+
+        peers = pl.ds(group * PACK_PEERS, PACK_PEERS)
+        pltpu.make_async_copy(packed.at[peers], out_ref.at[peers], out_sem).start()
+        return 0
+
+    lax.fori_loop(0, PACK_GROUPS, step, 0)
+    pltpu.make_async_copy(packed, out_ref, out_sem).wait()
 
 
 def pack(rank, x, v):
     return pl.pallas_call(
         pack_kernel,
-        grid_spec=pltpu.PrefetchScalarGridSpec(
-            num_scalar_prefetch=1,
-            grid=(GROUPS,),
-            in_specs=[
-                pl.BlockSpec((HALF, ROWS, LANES), lambda g, r: (0, jnp.maximum(g, r[0] // PEERS), 0)),
-                pl.BlockSpec((WIDTH, ROWS, LANES), lambda g, r: (0, jnp.minimum(g, r[0] // PEERS), 0)),
-            ],
-            out_specs=pl.BlockSpec((PEERS, BLOCK, LANES), lambda g, r: (g, 0, 0)),
-        ),
+        in_specs=[
+            pl.BlockSpec(memory_space=pltpu.SMEM),
+            pl.BlockSpec(memory_space=pl.ANY),
+            pl.BlockSpec(memory_space=pl.ANY),
+        ],
+        out_specs=pl.BlockSpec(memory_space=pl.ANY),
         out_shape=jax.ShapeDtypeStruct((DEVICES, BLOCK, LANES), jnp.float32),
+        scratch_shapes=[
+            pltpu.VMEM((PACK_GROUPS, HALF, PACK_ROWS, LANES), jnp.float32),
+            pltpu.VMEM((PACK_GROUPS, WIDTH, PACK_ROWS, LANES), jnp.float32),
+            pltpu.VMEM((DEVICES, BLOCK, LANES), jnp.float32),
+            pltpu.SemaphoreType.DMA((PACK_GROUPS,)),
+            pltpu.SemaphoreType.DMA((PACK_GROUPS,)),
+            pltpu.SemaphoreType.DMA,
+        ],
         compiler_params=pltpu.CompilerParams(vmem_limit_bytes=VMEM_LIMIT),
         cost_estimate=pl.CostEstimate(flops=0, bytes_accessed=12_000_000, transcendentals=0),
         name="pack",
@@ -166,64 +223,78 @@
     )(rank, x, v)
 
 
-def mirror_kernel(rank_ref, left_ref, received_ref, direct_ref, out_ref, below_ref, above_ref):
+def mirror_kernel(
+    rank_ref, left_ref, received_ref, direct_ref, out_ref, left, received, below_ref, above_ref, left_sem, received_sem
+):
     rank = rank_ref[0]
-    group = pl.program_id(0)
     own_group = rank // PEERS
 
-    @pl.when(group == 0)
-    def _():
-        below_ref[...] = jnp.zeros_like(below_ref)
-        above_ref[...] = jnp.zeros_like(above_ref)
-
-    def product(received):
-        right = jnp.concatenate(split(received), axis=1)
-        return dot(left_ref[0], right)
-
-    received = received_ref[...].reshape(TERMS, LANES)
-
-    @pl.when(group < own_group)
-    def _():
-        below_ref[...] += product(received)
-
-    @pl.when(group > own_group)
-    def _():
-        above_ref[...] += product(received)
-
-    @pl.when(group == own_group)
-    def _():
-        term = lax.broadcasted_iota(jnp.int32, (TERMS, LANES), 0)
-        first = (rank - group * PEERS) * BLOCK
-        below_ref[...] += product(jnp.where(term < first, received, 0.0))
-        above_ref[...] += product(jnp.where(term >= first + BLOCK, received, 0.0))
-
-    @pl.when(group == GROUPS - 1)
-    def _():
-        total = direct_ref[...] - (fold(above_ref[...]) + fold(below_ref[...]).T)
-        for row in range(ROW_DEVICES):
-            rows = total[OUT_ROWS * row : OUT_ROWS * (row + 1), :]
-            for col in range(COL_DEVICES):
-                out_ref[COL_DEVICES * row + col] = rows
+    def copies(turn):
+        group = lax.rem(own_group + turn, GROUPS)
+        peers = pl.ds(group * PEERS, PEERS)
+        return (
+            pltpu.make_async_copy(received_ref.at[peers], received.at[turn], received_sem.at[turn]),
+            pltpu.make_async_copy(left_ref.at[group], left.at[turn], left_sem.at[turn]),
+        )
+
+    for turn in range(GROUPS):
+        for copy in copies(turn):
+            copy.start()
+
+    def product(turn, values):
+        return dot(left[turn], jnp.concatenate(split(values), axis=1))
+
+    for copy in copies(0):
+        copy.wait()
+    values = received[0].reshape(TERMS, LANES)
+    term = lax.broadcasted_iota(jnp.int32, (TERMS, LANES), 0)
+    first = (rank - own_group * PEERS) * BLOCK
+    below_ref[...] = product(0, jnp.where(term < first, values, 0.0))
+    above_ref[...] = product(0, jnp.where(term >= first + BLOCK, values, 0.0))
+
+    def step(turn, _):
+        for copy in copies(turn):
+            copy.wait()
+        values = received[turn].reshape(TERMS, LANES)
+        below = own_group + turn >= GROUPS
+
+        @pl.when(below)
+        def _():
+            below_ref[...] += product(turn, values)
+
+        @pl.when(jnp.logical_not(below))
+        def _():
+            above_ref[...] += product(turn, values)
+
+        return 0
+
+    lax.fori_loop(1, GROUPS, step, 0)
+    total = direct_ref[...] - (fold(above_ref[...]) + fold(below_ref[...]).T)
+    for row in range(ROW_DEVICES):
+        rows = total[OUT_ROWS * row : OUT_ROWS * (row + 1), :]
+        for col in range(COL_DEVICES):
+            out_ref[COL_DEVICES * row + col] = rows
 
 
 def mirror(rank, left, received, direct):
     return pl.pallas_call(
         mirror_kernel,
-        grid_spec=pltpu.PrefetchScalarGridSpec(
-            num_scalar_prefetch=1,
-            grid=(GROUPS,),
-            in_specs=[
-                pl.BlockSpec((1, 2 * LANES, TERMS), lambda g, r: (g, 0, 0)),
-                pl.BlockSpec((PEERS, BLOCK, LANES), lambda g, r: (g, 0, 0)),
-                pl.BlockSpec((LANES, LANES), lambda g, r: (0, 0)),
-            ],
-            out_specs=pl.BlockSpec((DEVICES, OUT_ROWS, LANES), lambda g, r: (0, 0, 0)),
-            scratch_shapes=[
-                pltpu.VMEM((2 * LANES, 2 * LANES), jnp.float32),
-                pltpu.VMEM((2 * LANES, 2 * LANES), jnp.float32),
-            ],
-        ),
+        in_specs=[
+            pl.BlockSpec(memory_space=pltpu.SMEM),
+            pl.BlockSpec(memory_space=pl.ANY),
+            pl.BlockSpec(memory_space=pl.ANY),
+            pl.BlockSpec(memory_space=pltpu.VMEM),
+        ],
+        out_specs=pl.BlockSpec(memory_space=pltpu.VMEM),
         out_shape=jax.ShapeDtypeStruct((DEVICES, OUT_ROWS, LANES), jnp.float32),
+        scratch_shapes=[
+            pltpu.VMEM((GROUPS, 2 * LANES, TERMS), jnp.bfloat16),
+            pltpu.VMEM((GROUPS, PEERS, BLOCK, LANES), jnp.float32),
+            pltpu.VMEM((2 * LANES, 2 * LANES), jnp.float32),
+            pltpu.VMEM((2 * LANES, 2 * LANES), jnp.float32),
+            pltpu.SemaphoreType.DMA((GROUPS,)),
+            pltpu.SemaphoreType.DMA((GROUPS,)),
+        ],
         compiler_params=pltpu.CompilerParams(vmem_limit_bytes=VMEM_LIMIT),
         cost_estimate=pl.CostEstimate(flops=2_500_000_000, bytes_accessed=10_000_000, transcendentals=0),
         name="mirror",

time: 108 us -> 102 us (0.944)
  Pallas kernels: 26.9 us -> 20 us
    pallas_call x2, Pallas kernels: 16.3 us -> 10.1 us  [the longest x1 6.09 us: mirror(): pl.pallas_call(mirror_kernel, in_specs=[pl.BlockSpec(memory_space=pltpu.S...]
where the time goes in v2:
time: 102 us
  waiting for transfers between devices  48 us (47%)
  Pallas kernels  20 us (20%)
  blocking collectives  19.5 us (19%)
  starting transfers between devices  13.5 us (13%)
    all_to_all x1, waiting for transfers between devices, body(): received = lax.all_to_all(pack(rank, x, v), AXES, 0, 0, tiled=True)  48 us
    all_to_all x1, blocking collectives, body(): lax.all_to_all(mirror(rank, left, received, direct), AXES, 0, 0, tiled=True)  19.5 us
    all_to_all x1, starting transfers between devices, body(): received = lax.all_to_all(pack(rank, x, v), AXES, 0, 0, tiled=True)  13.5 us
    pallas_call x1, Pallas kernels, local(): pl.pallas_call(local_kernel, grid_spec=pltpu.PrefetchScalarGridSpec(num_s...  9.88 us
    pallas_call x1, Pallas kernels, mirror(): pl.pallas_call(mirror_kernel, in_specs=[pl.BlockSpec(memory_space=pltpu.S...  6.09 us
    pallas_call x1, Pallas kernels, pack(): pl.pallas_call(pack_kernel, in_specs=[pl.BlockSpec(memory_space=pltpu.SME...  4.02 us
  transfers between devices with their start and end apart: 1, of which 1 were waited for; matrix products, arithmetic and copies ran while one was open for 0% of the time, Pallas kernels for 10%

profile of v2, /device:TPU:0, one launch (start us, length us, event | category | flops | bytes accessed | tf_op | source)
XLA Modules:
  0.0 101.7 jit_solution(7673059114393033095)
XLA Ops:
  0.0 4.0 %pack.1 = f32[128,72,128]{2,1,0:T(8,128)} custom-call(s32[1]{0:T(128)} %bitcast.rank_ref, f32[12,1536,128]{2,1,0:T(8,128)} %bitcast.3, f32[12,1536,128]{2,1,0:T(8,128)} %bitcast.5), custom_call_target="tpu_custom_call" | custom-call | bytes 12000000 | tf_op jit(solution)/shard_map/pack/pallas_call | solution.py:115
  4.0 13.5 %all-to-all-start = ((f32[128,72,128]{2,1,0:T(8,128)}), f32[128,72,128]{2,1,0:T(8,128)}, u32[]{:S(2)}, u32[]{:S(2)}) async-start(f32[128,72,128]{2,1,0:T(8,128)} %pack.1), calls=%async_computation | async-start | bytes 9437184 | tf_op jit(solution)/shard_map/all_to_all | solution.py:308
  17.5 9.9 %local.1 = (bf16[4,256,2304]{2,1,0:T(8,128)(2,1)}, f32[128,128]{1,0:T(8,128)}) custom-call(s32[1]{0:T(128)} %bitcast.rank_ref, f32[12,1536,128]{2,1,0:T(8,128)} %bitcast.4, f32[12,1536,128]{2,1,0:T(8,128)} %bitcast.6), custom_call_target="tpu_custom_call" | custom-call | flops 20000000000 | bytes 30000000 | tf_op jit(solution)/shard_map/local/pallas_call | solution.py:196
  27.4 48.0 %all-to-all-done.received_ref = f32[128,72,128]{2,1,0:T(8,128)} async-done(((f32[128,72,128]{2,1,0:T(8,128)}), f32[128,72,128]{2,1,0:T(8,128)}, u32[]{:S(2)}, u32[]{:S(2)}) %all-to-all-start) | async-done | bytes 4718624 | tf_op jit(solution)/shard_map/all_to_all | solution.py:308
  75.3 6.1 %mirror.1 = f32[128,8,128]{2,1,0:T(8,128)} custom-call(s32[1]{0:T(128)} %bitcast.rank_ref, bf16[4,256,2304]{2,1,0:T(8,128)(2,1)} %get-tuple-element.7.left_ref, f32[128,72,128]{2,1,0:T(8,128)} %all-to-all-done.received_ref, f32[128,128]{1,0:T(8,128)} %get-tuple-element.8.direct_ref), custom_call_target="tpu_custom_call" | custom-call | flops 2500000000 | bytes 10000000 | tf_op jit(solution)/shard_map/mirror/pallas_call | solution.py:280
  81.4 19.5 %all_to_all.10 = f32[128,8,128]{2,1,0:T(8,128)S(1)} all-to-all(f32[128,8,128]{2,1,0:T(8,128)} %mirror.1), channel_id=1, replica_groups=mesh['row'=16,'col'=8] {'row','col'}, dimensions={0} | all-to-all | bytes 1048576 | tf_op jit(solution)/shard_map/all_to_all | solution.py:310
  100.9 0.7 reduce_sum.9
Async XLA Ops:
  4.0 71.3 %all-to-all-start = ((f32[128,72,128]{2,1,0:T(8,128)}), f32[128,72,128]{2,1,0:T(8,128)}, u32[]{:S(2)}, u32[]{:S(2)}) async-start(f32[128,72,128]{2,1,0:T(8,128)} %pack.1), calls=%async_computation | async-start | bytes 9437184 | tf_op jit(solution)/shard_map/all_to_all | solution.py:308

commit v3 on v2

--- a/solution.py
+++ b/solution.py
@@ -16,12 +16,15 @@
 PACK_ROWS = PACK_PEERS * WIDTH
 PEERS = 32
 GROUPS = DEVICES // PEERS
+LEFT_GROUPS = 20
+DIRECT_LENGTH = 320
 ROWS = PEERS * WIDTH
 TERMS = PEERS * BLOCK
 ROW_DEVICES = 16
 COL_DEVICES = 8
 OUT_ROWS = LANES // ROW_DEVICES
 VMEM_LIMIT = 56 * 1024 * 1024
+MIRROR_VMEM_LIMIT = 44 * 1024 * 1024
 
 
 def split(value):
@@ -39,72 +42,82 @@
     return top + (acc[LANES:, :LANES] + acc[LANES:, LANES:])
 
 
-def pack_kernel(rank_ref, x_ref, v_ref, out_ref, x_rows, v_rows, packed, x_sem, v_sem, out_sem):
+def pack_kernel(rank_ref, x_ref, v_ref, out_ref, rows_ref, own_ref, packed, in_sem, own_sem, out_sem):
     rank = rank_ref[0]
     own_group = rank // PACK_PEERS
-
-    def x_copy(group):
-        rows = pl.ds(group * PACK_ROWS, PACK_ROWS)
-        return pltpu.make_async_copy(x_ref.at[pl.ds(0, HALF), rows], x_rows.at[group], x_sem.at[group])
-
-    def v_copy(group):
-        rows = pl.ds(group * PACK_ROWS, PACK_ROWS)
-        return pltpu.make_async_copy(v_ref.at[:, rows], v_rows.at[group], v_sem.at[group])
-
-    def pack_x(group, i):
-        for c in range(HALF):
-            rows = x_rows[group, c, pl.ds(WIDTH * i, WIDTH), :]
-            packed[group * PACK_PEERS + i, pl.ds(WIDTH * c, WIDTH), :] = rows
-
-    def pack_v(group, i):
-        for d in range(WIDTH):
-            rows = v_rows[group, d, pl.ds(WIDTH * i + HALF, HALF), :]
-            packed[group * PACK_PEERS + i, pl.ds(HALF * d, HALF), :] = rows
-
+    first, last, whole = pl.ds(0, HALF), pl.ds(HALF, HALF), pl.ds(0, WIDTH)
+
+    def read(ref, columns, group):
+        source = ref.at[columns, pl.ds(group * PACK_ROWS, PACK_ROWS)]
+        return pltpu.make_async_copy(source, rows_ref.at[group, columns], in_sem.at[group])
+
+    def read_own():
+        source = v_ref.at[whole, pl.ds(own_group * PACK_ROWS, PACK_ROWS)]
+        return pltpu.make_async_copy(source, own_ref, own_sem)
+
+    def whole_rows(group, i, columns):
+        for n, c in enumerate(columns):
+            packed[group * PACK_PEERS + i, pl.ds(WIDTH * n, WIDTH), :] = rows_ref[group, c, pl.ds(WIDTH * i, WIDTH), :]
+
+    def half_rows(group, i, start):
+        for c in range(WIDTH):
+            packed[group * PACK_PEERS + i, pl.ds(HALF * c, HALF), :] = rows_ref[
+                group, c, pl.ds(WIDTH * i + start, HALF), :
+            ]
+
+    def cases(group):
+        above = group > own_group
+        below = group < own_group
+        odd = lax.rem(group + own_group, 2) == 1
+        even = jnp.logical_not(odd)
+        return (
+            (jnp.logical_and(above, even), x_ref, first, lambda i: whole_rows(group, i, range(HALF))),
+            (jnp.logical_and(above, odd), x_ref, whole, lambda i: half_rows(group, i, 0)),
+            (jnp.logical_and(below, odd), v_ref, last, lambda i: whole_rows(group, i, range(HALF, WIDTH))),
+            (jnp.logical_and(below, even), v_ref, whole, lambda i: half_rows(group, i, HALF)),
+        )
+
+    read(x_ref, first, own_group).start()
+    read_own().start()
     for group in range(PACK_GROUPS):
-
-        @pl.when(group >= own_group)
-        def _():
-            x_copy(group).start()
-
-        @pl.when(group <= own_group)
-        def _():
-            v_copy(group).start()
-
-    def step(group, _):
-        @pl.when(group >= own_group)
-        def _():
-            x_copy(group).wait()
-
-        @pl.when(group <= own_group)
-        def _():
-            v_copy(group).wait()
-
-        @pl.when(group > own_group)
-        def _():
-            for i in range(PACK_PEERS):
-                pack_x(group, i)
-
-        @pl.when(group < own_group)
-        def _():
-            for i in range(PACK_PEERS):
-                pack_v(group, i)
-
-        @pl.when(group == own_group)
-        def _():
-            for i in range(PACK_PEERS):
-                below = group * PACK_PEERS + i < rank
-
-                @pl.when(below)
-                def _():
-                    pack_v(group, i)
-
-                @pl.when(jnp.logical_not(below))
-                def _():
-                    pack_x(group, i)
-
+        for condition, ref, columns, _ in cases(group):
+
+            @pl.when(condition)
+            def _():
+                read(ref, columns, group).start()
+
+    def write(group):
         peers = pl.ds(group * PACK_PEERS, PACK_PEERS)
         pltpu.make_async_copy(packed.at[peers], out_ref.at[peers], out_sem).start()
+
+    read(x_ref, first, own_group).wait()
+    read_own().wait()
+    for i in range(PACK_PEERS):
+        below = own_group * PACK_PEERS + i < rank
+
+        @pl.when(below)
+        def _():
+            for d in range(WIDTH):
+                packed[own_group * PACK_PEERS + i, pl.ds(HALF * d, HALF), :] = own_ref[
+                    d, pl.ds(WIDTH * i + HALF, HALF), :
+                ]
+
+        @pl.when(jnp.logical_not(below))
+        def _():
+            whole_rows(own_group, i, range(HALF))
+
+    write(own_group)
+
+    def step(group, _):
+        for condition, ref, columns, move in cases(group):
+
+            @pl.when(condition)
+            def _():
+                read(ref, columns, group).wait()
+                for i in range(PACK_PEERS):
+                    move(i)
+                write(group)
+
         return 0
 
     lax.fori_loop(0, PACK_GROUPS, step, 0)
@@ -122,11 +135,11 @@
         out_specs=pl.BlockSpec(memory_space=pl.ANY),
         out_shape=jax.ShapeDtypeStruct((DEVICES, BLOCK, LANES), jnp.float32),
         scratch_shapes=[
-            pltpu.VMEM((PACK_GROUPS, HALF, PACK_ROWS, LANES), jnp.float32),
             pltpu.VMEM((PACK_GROUPS, WIDTH, PACK_ROWS, LANES), jnp.float32),
+            pltpu.VMEM((WIDTH, PACK_ROWS, LANES), jnp.float32),
             pltpu.VMEM((DEVICES, BLOCK, LANES), jnp.float32),
             pltpu.SemaphoreType.DMA((PACK_GROUPS,)),
-            pltpu.SemaphoreType.DMA((PACK_GROUPS,)),
+            pltpu.SemaphoreType.DMA,
             pltpu.SemaphoreType.DMA,
         ],
         compiler_params=pltpu.CompilerParams(vmem_limit_bytes=VMEM_LIMIT),
@@ -144,18 +157,33 @@
     def _():
         acc_ref[...] = jnp.zeros_like(acc_ref)
 
+    own_pack_group = rank // PACK_PEERS
     for i in range(PEERS):
         peer = group * PEERS + i
-
-        @pl.when(peer > rank)
+        odd = lax.rem(group * (PEERS // PACK_PEERS) + i // PACK_PEERS + own_pack_group, 2) == 1
+        even = jnp.logical_not(odd)
+        above = peer > rank
+        below = peer < rank
+
+        @pl.when(jnp.logical_and(above, even))
         def _():
             for c in range(HALF):
                 terms_ref[pl.ds(BLOCK * i + c, WIDTH, stride=HALF), :] = x_ref[HALF + c, pl.ds(WIDTH * i, WIDTH), :]
 
-        @pl.when(peer < rank)
+        @pl.when(jnp.logical_and(above, odd))
+        def _():
+            for c in range(WIDTH):
+                terms_ref[pl.ds(BLOCK * i + c, HALF, stride=WIDTH), :] = x_ref[c, pl.ds(WIDTH * i + HALF, HALF), :]
+
+        @pl.when(jnp.logical_and(below, even))
         def _():
             for d in range(WIDTH):
                 terms_ref[pl.ds(BLOCK * i + d, HALF, stride=WIDTH), :] = v_ref[d, pl.ds(WIDTH * i, HALF), :]
+
+        @pl.when(jnp.logical_and(below, odd))
+        def _():
+            for d in range(HALF):
+                terms_ref[pl.ds(BLOCK * i + d, WIDTH, stride=HALF), :] = v_ref[d, pl.ds(WIDTH * i, WIDTH), :]
 
         @pl.when(peer == rank)
         def _():
@@ -189,7 +217,7 @@
 
     @pl.when(group == GROUPS - 1)
     def _():
-        direct_ref[...] = fold(acc_ref[...])
+        direct_ref[0] = fold(acc_ref[...])
 
 
 def local(rank, x, v):
@@ -204,7 +232,7 @@
             ],
             out_specs=[
                 pl.BlockSpec((1, 2 * LANES, TERMS), lambda g, r: (g, 0, 0)),
-                pl.BlockSpec((LANES, LANES), lambda g, r: (0, 0)),
+                pl.BlockSpec((1, LANES, LANES), lambda g, r: (0, 0, 0)),
             ],
             scratch_shapes=[
                 pltpu.VMEM((TERMS, LANES), jnp.float32),
@@ -214,8 +242,8 @@
             ],
         ),
         out_shape=[
-            jax.ShapeDtypeStruct((GROUPS, 2 * LANES, TERMS), jnp.bfloat16),
-            jax.ShapeDtypeStruct((LANES, LANES), jnp.float32),
+            jax.ShapeDtypeStruct((LEFT_GROUPS, 2 * LANES, TERMS), jnp.bfloat16),
+            jax.ShapeDtypeStruct((DIRECT_LENGTH, LANES, LANES), jnp.float32),
         ],
         compiler_params=pltpu.CompilerParams(vmem_limit_bytes=VMEM_LIMIT),
         cost_estimate=pl.CostEstimate(flops=20_000_000_000, bytes_accessed=30_000_000, transcendentals=0),
@@ -224,7 +252,19 @@
 
 
 def mirror_kernel(
-    rank_ref, left_ref, received_ref, direct_ref, out_ref, left, received, below_ref, above_ref, left_sem, received_sem
+    rank_ref,
+    left_ref,
+    received_ref,
+    direct_ref,
+    out_ref,
+    left,
+    received,
+    direct,
+    below_ref,
+    above_ref,
+    left_sem,
+    received_sem,
+    direct_sem,
 ):
     rank = rank_ref[0]
     own_group = rank // PEERS
@@ -240,6 +280,8 @@
     for turn in range(GROUPS):
         for copy in copies(turn):
             copy.start()
+    direct_copy = pltpu.make_async_copy(direct_ref.at[0], direct, direct_sem)
+    direct_copy.start()
 
     def product(turn, values):
         return dot(left[turn], jnp.concatenate(split(values), axis=1))
@@ -269,7 +311,8 @@
         return 0
 
     lax.fori_loop(1, GROUPS, step, 0)
-    total = direct_ref[...] - (fold(above_ref[...]) + fold(below_ref[...]).T)
+    direct_copy.wait()
+    total = direct[...] - (fold(above_ref[...]) + fold(below_ref[...]).T)
     for row in range(ROW_DEVICES):
         rows = total[OUT_ROWS * row : OUT_ROWS * (row + 1), :]
         for col in range(COL_DEVICES):
@@ -283,19 +326,21 @@
             pl.BlockSpec(memory_space=pltpu.SMEM),
             pl.BlockSpec(memory_space=pl.ANY),
             pl.BlockSpec(memory_space=pl.ANY),
-            pl.BlockSpec(memory_space=pltpu.VMEM),
+            pl.BlockSpec(memory_space=pl.ANY),
         ],
         out_specs=pl.BlockSpec(memory_space=pltpu.VMEM),
         out_shape=jax.ShapeDtypeStruct((DEVICES, OUT_ROWS, LANES), jnp.float32),
         scratch_shapes=[
             pltpu.VMEM((GROUPS, 2 * LANES, TERMS), jnp.bfloat16),
             pltpu.VMEM((GROUPS, PEERS, BLOCK, LANES), jnp.float32),
+            pltpu.VMEM((LANES, LANES), jnp.float32),
             pltpu.VMEM((2 * LANES, 2 * LANES), jnp.float32),
             pltpu.VMEM((2 * LANES, 2 * LANES), jnp.float32),
             pltpu.SemaphoreType.DMA((GROUPS,)),
             pltpu.SemaphoreType.DMA((GROUPS,)),
-        ],
-        compiler_params=pltpu.CompilerParams(vmem_limit_bytes=VMEM_LIMIT),
+            pltpu.SemaphoreType.DMA,
+        ],
+        compiler_params=pltpu.CompilerParams(vmem_limit_bytes=MIRROR_VMEM_LIMIT),
         cost_estimate=pl.CostEstimate(flops=2_500_000_000, bytes_accessed=10_000_000, transcendentals=0),
         name="mirror",
     )(rank, left, received, direct)

time: 102 us -> 100 us (0.980)
  starting transfers between devices: 13.5 us -> 11.6 us
    all_to_all x1, starting transfers between devices: 13.5 us -> 11.6 us  [body(): received = lax.all_to_all(pack(rank, x, v), AXES, 0, 0, tiled=True)]
    pallas_call x1, Pallas kernels: 4.02 us -> 5.74 us  [pack(): pl.pallas_call(pack_kernel, in_specs=[pl.BlockSpec(memory_space=pltpu.SME...]
    pallas_call x1, Pallas kernels: 6.09 us -> 4.45 us  [mirror(): pl.pallas_call(mirror_kernel, in_specs=[pl.BlockSpec(memory_space=pltpu.S...]
  transfers between devices with their start and end apart: 1 -> 1, of which waited for: 1 -> 1; matrix products, arithmetic and copies ran while one was open for 0% -> 0% of each run, Pallas kernels for 10% -> 11%
where the time goes in v3:
time: 100 us; the launch traced here: 99.7 us
  waiting for transfers between devices  47.2 us (47%)
  Pallas kernels  20.9 us (21%)
  blocking collectives  19.3 us (19%)
  starting transfers between devices  11.6 us (12%)
    all_to_all x1, waiting for transfers between devices, body(): received = lax.all_to_all(pack(rank, x, v), AXES, 0, 0, tiled=True)  47.2 us
    all_to_all x1, blocking collectives, body(): lax.all_to_all(mirror(rank, left, received, direct), AXES, 0, 0, tiled=True)  19.3 us
    all_to_all x1, starting transfers between devices, body(): received = lax.all_to_all(pack(rank, x, v), AXES, 0, 0, tiled=True)  11.6 us
    pallas_call x1, Pallas kernels, local(): pl.pallas_call(local_kernel, grid_spec=pltpu.PrefetchScalarGridSpec(num_s...  10.7 us
    pallas_call x1, Pallas kernels, pack(): pl.pallas_call(pack_kernel, in_specs=[pl.BlockSpec(memory_space=pltpu.SME...  5.74 us
    pallas_call x1, Pallas kernels, mirror(): pl.pallas_call(mirror_kernel, in_specs=[pl.BlockSpec(memory_space=pltpu.S...  4.45 us
  transfers between devices with their start and end apart: 1, of which 1 were waited for; matrix products, arithmetic and copies ran while one was open for 0% of the time, Pallas kernels for 11%

profile of v3, /device:TPU:0, one launch (start us, length us, event | category | flops | bytes accessed | tf_op | source)
XLA Modules:
  0.0 99.7 jit_solution(974434734972556903)
XLA Ops:
  0.0 5.7 %pack.1 = f32[128,72,128]{2,1,0:T(8,128)} custom-call(s32[1]{0:T(128)} %bitcast.rank_ref, f32[12,1536,128]{2,1,0:T(8,128)} %bitcast.3, f32[12,1536,128]{2,1,0:T(8,128)} %bitcast.5), custom_call_target="tpu_custom_call" | custom-call | bytes 12000000 | tf_op jit(solution)/shard_map/pack/pallas_call | solution.py:128
  5.8 11.6 %all-to-all-start = ((f32[128,72,128]{2,1,0:T(8,128)}), f32[128,72,128]{2,1,0:T(8,128)}, u32[]{:S(2)}, u32[]{:S(2)}) async-start(f32[128,72,128]{2,1,0:T(8,128)} %pack.1), calls=%async_computation | async-start | bytes 9437184 | tf_op jit(solution)/shard_map/all_to_all | solution.py:353
  17.4 10.7 %local.1 = (bf16[20,256,2304]{2,1,0:T(8,128)(2,1)}, f32[320,128,128]{2,1,0:T(8,128)}) custom-call(s32[1]{0:T(128)} %bitcast.rank_ref, f32[12,1536,128]{2,1,0:T(8,128)} %bitcast.4, f32[12,1536,128]{2,1,0:T(8,128)} %bitcast.6), custom_call_target="tpu_custom_call" | custom-call | flops 20000000000 | bytes 30000000 | tf_op jit(solution)/shard_map/local/pallas_call | solution.py:224
  28.1 47.2 %all-to-all-done.received_ref = f32[128,72,128]{2,1,0:T(8,128)} async-done(((f32[128,72,128]{2,1,0:T(8,128)}), f32[128,72,128]{2,1,0:T(8,128)}, u32[]{:S(2)}, u32[]{:S(2)}) %all-to-all-start) | async-done | bytes 4718624 | tf_op jit(solution)/shard_map/all_to_all | solution.py:353
  75.2 4.5 %mirror.1 = f32[128,8,128]{2,1,0:T(8,128)S(1)} custom-call(s32[1]{0:T(128)} %bitcast.rank_ref, bf16[20,256,2304]{2,1,0:T(8,128)(2,1)} %get-tuple-element.7.left_ref, f32[128,72,128]{2,1,0:T(8,128)} %all-to-all-done.received_ref, f32[320,128,128]{2,1,0:T(8,128)} %get-tuple-element.8.direct_ref), custom_call_target="tpu_custom_call" | custom-call | flops 2500000000 | bytes 10000000 | tf_op jit(solution)/shard_map/mirror/pallas_call | solution.py:323
  79.7 19.3 %all_to_all.10 = f32[128,8,128]{2,1,0:T(8,128)S(1)} all-to-all(f32[128,8,128]{2,1,0:T(8,128)S(1)} %mirror.1), channel_id=1, replica_groups=mesh['row'=16,'col'=8] {'row','col'}, dimensions={0} | all-to-all | bytes 1048576 | tf_op jit(solution)/shard_map/all_to_all | solution.py:355
  99.0 0.7 reduce_sum.9
Async XLA Ops:
  5.8 69.5 %all-to-all-start = ((f32[128,72,128]{2,1,0:T(8,128)}), f32[128,72,128]{2,1,0:T(8,128)}, u32[]{:S(2)}, u32[]{:S(2)}) async-start(f32[128,72,128]{2,1,0:T(8,128)} %pack.1), calls=%async_computation | async-start | bytes 9437184 | tf_op jit(solution)/shard_map/all_to_all | solution.py:353

commit v4 on v3

--- a/solution.py
+++ b/solution.py
@@ -3,9 +3,11 @@
 from jax import lax
 from jax.experimental import pallas as pl
 from jax.experimental.pallas import tpu as pltpu
+from jax.sharding import Mesh
 from jax.sharding import PartitionSpec as P
 
-AXES = ("row", "col")
+AXES = ("half", "core", "col")
+CHIPS = ("half", "col")
 DEVICES = 128
 WIDTH = 12
 HALF = WIDTH // 2
@@ -20,9 +22,10 @@
 DIRECT_LENGTH = 320
 ROWS = PEERS * WIDTH
 TERMS = PEERS * BLOCK
-ROW_DEVICES = 16
+CORES = 2
+HALVES = 8
 COL_DEVICES = 8
-OUT_ROWS = LANES // ROW_DEVICES
+OUT_ROWS = LANES // (HALVES * CORES)
 VMEM_LIMIT = 56 * 1024 * 1024
 MIRROR_VMEM_LIMIT = 44 * 1024 * 1024
 
@@ -256,7 +259,8 @@
     left_ref,
     received_ref,
     direct_ref,
-    out_ref,
+    mine_ref,
+    other_ref,
     left,
     received,
     direct,
@@ -313,10 +317,13 @@
     lax.fori_loop(1, GROUPS, step, 0)
     direct_copy.wait()
     total = direct[...] - (fold(above_ref[...]) + fold(below_ref[...]).T)
-    for row in range(ROW_DEVICES):
-        rows = total[OUT_ROWS * row : OUT_ROWS * (row + 1), :]
-        for col in range(COL_DEVICES):
-            out_ref[COL_DEVICES * row + col] = rows
+    first_core = lax.rem(rank // COL_DEVICES, CORES) == 0
+    for half in range(HALVES):
+        start = half * CORES * OUT_ROWS
+        zero = total[start : start + OUT_ROWS, :]
+        one = total[start + OUT_ROWS : start + 2 * OUT_ROWS, :]
+        mine_ref[half] = jnp.where(first_core, zero, one)
+        other_ref[half] = jnp.where(first_core, one, zero)
 
 
 def mirror(rank, left, received, direct):
@@ -328,8 +335,8 @@
             pl.BlockSpec(memory_space=pl.ANY),
             pl.BlockSpec(memory_space=pl.ANY),
         ],
-        out_specs=pl.BlockSpec(memory_space=pltpu.VMEM),
-        out_shape=jax.ShapeDtypeStruct((DEVICES, OUT_ROWS, LANES), jnp.float32),
+        out_specs=[pl.BlockSpec(memory_space=pltpu.VMEM)] * 2,
+        out_shape=[jax.ShapeDtypeStruct((HALVES, OUT_ROWS, LANES), jnp.float32)] * 2,
         scratch_shapes=[
             pltpu.VMEM((GROUPS, 2 * LANES, TERMS), jnp.bfloat16),
             pltpu.VMEM((GROUPS, PEERS, BLOCK, LANES), jnp.float32),
@@ -349,18 +356,22 @@
 def body(cycle_inter, integrals):
     x = jnp.swapaxes(cycle_inter, 0, 1)
     v = jnp.swapaxes(integrals, 0, 1)
-    rank = (lax.axis_index("row") * lax.axis_size("col") + lax.axis_index("col")).astype(jnp.int32).reshape(1)
+    rank = lax.axis_index(AXES).astype(jnp.int32).reshape(1)
     received = lax.all_to_all(pack(rank, x, v), AXES, 0, 0, tiled=True)
     left, direct = local(rank, x, v)
-    parts = lax.all_to_all(mirror(rank, left, received, direct), AXES, 0, 0, tiled=True)
-    return jnp.sum(parts, axis=0)
+    mine, other = mirror(rank, left, received, direct)
+    rows = mine + lax.ppermute(other, "core", [(0, 1), (1, 0)])
+    parts = jnp.broadcast_to(rows[:, None], (HALVES, COL_DEVICES, OUT_ROWS, LANES))
+    parts = parts.reshape(HALVES * COL_DEVICES, OUT_ROWS, LANES)
+    return jnp.sum(lax.all_to_all(parts, CHIPS, 0, 0, tiled=True), axis=0)
 
 
 def solution(mesh):
+    cores = Mesh(mesh.devices.reshape(HALVES, CORES, COL_DEVICES), AXES)
     return jax.shard_map(
         body,
-        mesh=mesh,
+        mesh=cores,
         in_specs=(P(None, AXES, None), P(None, AXES, None)),
-        out_specs=P("row", None),
+        out_specs=P(("half", "core"), None),
         check_vma=False,
     )

time: 100 us -> 98.6 us (0.986)
  blocking collectives: 19.3 us -> 16.6 us
  waiting for transfers between devices: 47.2 us -> 48.4 us
    all_to_all x1, blocking collectives: 19.3 us -> 16.6 us  [body(): return jnp.sum(lax.all_to_all(parts, CHIPS, 0, 0, tiled=True), axis=0)]
    ppermute x0 -> x1, waiting for transfers between devices: none -> 1.19 us  [body(): rows = mine + lax.ppermute(other, 'core', [(0, 1), (1, 0)])]
  transfers between devices with their start and end apart: 1 -> 2, of which waited for: 1 -> 2; matrix products, arithmetic and copies ran while one was open for 0% -> 0% of each run, Pallas kernels for 11% -> 11%
where the time goes in v4:
time: 98.6 us; the launch traced here: 98.3 us
  waiting for transfers between devices  48.4 us (49%)
  Pallas kernels  20.9 us (21%)
  blocking collectives  16.6 us (17%)
  starting transfers between devices  11.7 us (12%)
    all_to_all x1, waiting for transfers between devices, body(): received = lax.all_to_all(pack(rank, x, v), AXES, 0, 0, tiled=True)  47.2 us
    all_to_all x1, blocking collectives, body(): return jnp.sum(lax.all_to_all(parts, CHIPS, 0, 0, tiled=True), axis=0)  16.6 us
    all_to_all x1, starting transfers between devices, body(): received = lax.all_to_all(pack(rank, x, v), AXES, 0, 0, tiled=True)  11.6 us
    pallas_call x1, Pallas kernels, local(): pl.pallas_call(local_kernel, grid_spec=pltpu.PrefetchScalarGridSpec(num_s...  10.7 us
    pallas_call x1, Pallas kernels, pack(): pl.pallas_call(pack_kernel, in_specs=[pl.BlockSpec(memory_space=pltpu.SME...  5.75 us
    pallas_call x1, Pallas kernels, mirror(): pl.pallas_call(mirror_kernel, in_specs=[pl.BlockSpec(memory_space=pltpu.S...  4.47 us
  transfers between devices with their start and end apart: 2, of which 2 were waited for; matrix products, arithmetic and copies ran while one was open for 0% of the time, Pallas kernels for 11%

profile of v4, /device:TPU:0, one launch (start us, length us, event | category | flops | bytes accessed | tf_op | source)
XLA Modules:
  0.0 98.3 jit_solution(803636169153370161)
XLA Ops:
  0.0 5.8 %pack.1 = f32[128,72,128]{2,1,0:T(8,128)} custom-call(s32[1]{0:T(128)} %bitcast.rank_ref, f32[12,1536,128]{2,1,0:T(8,128)} %bitcast.4, f32[12,1536,128]{2,1,0:T(8,128)} %bitcast.6), custom_call_target="tpu_custom_call" | custom-call | bytes 12000000 | tf_op jit(solution)/shard_map/pack/pallas_call | solution.py:131
  5.8 11.6 %all-to-all-start = ((f32[128,72,128]{2,1,0:T(8,128)}), f32[128,72,128]{2,1,0:T(8,128)}, u32[]{:S(2)}, u32[]{:S(2)}) async-start(f32[128,72,128]{2,1,0:T(8,128)} %pack.1), calls=%async_computation | async-start | bytes 9437184 | tf_op jit(solution)/shard_map/all_to_all | solution.py:360
  17.4 10.7 %local.1 = (bf16[20,256,2304]{2,1,0:T(8,128)(2,1)}, f32[320,128,128]{2,1,0:T(8,128)}) custom-call(s32[1]{0:T(128)} %bitcast.rank_ref, f32[12,1536,128]{2,1,0:T(8,128)} %bitcast.5, f32[12,1536,128]{2,1,0:T(8,128)} %bitcast.7), custom_call_target="tpu_custom_call" | custom-call | flops 20000000000 | bytes 30000000 | tf_op jit(solution)/shard_map/local/pallas_call | solution.py:227
  28.0 47.2 %all-to-all-done.received_ref = f32[128,72,128]{2,1,0:T(8,128)} async-done(((f32[128,72,128]{2,1,0:T(8,128)}), f32[128,72,128]{2,1,0:T(8,128)}, u32[]{:S(2)}, u32[]{:S(2)}) %all-to-all-start) | async-done | bytes 4718624 | tf_op jit(solution)/shard_map/all_to_all | solution.py:360
  75.2 4.5 %mirror.1 = (f32[8,8,128]{2,1,0:T(8,128)S(1)}, f32[8,8,128]{2,1,0:T(8,128)S(1)}) custom-call(s32[1]{0:T(128)} %bitcast.rank_ref, bf16[20,256,2304]{2,1,0:T(8,128)(2,1)} %get-tuple-element.9.left_ref, f32[128,72,128]{2,1,0:T(8,128)} %all-to-all-done.received_ref, f32[320,128,128]{2,1,0:T(8,128)} %get-tuple-element.10.direct_ref), custom_call_target="tpu_custom_call" | custom-call | flops 2500000000 | bytes 10000000 | tf_op jit(solution)/shard_map/mirror/pallas_call | solution.py:330
  79.7 0.1 collective-permute-start
  79.8 1.2 %collective-permute-done = f32[8,8,128]{2,1,0:T(8,128)S(1)} collective-permute-done((f32[8,8,128]{2,1,0:T(8,128)S(1)}, f32[8,8,128]{2,1,0:T(8,128)S(1)}, u32[]{:S(2)}, u32[]{:S(2)}) %collective-permute-start) | collective-permute-done | bytes 32800 | tf_op jit(solution)/shard_map/ppermute | solution.py:363
  81.0 16.6 %all_to_all.10 = f32[64,8,128]{2,1,0:T(8,128)S(1)} all-to-all(f32[64,8,128]{2,1,0:T(8,128)S(1)} %bitcast.8), channel_id=1, replica_groups=mesh['half'=8,'core'=2,'col'=8] {'half','col'}, dimensions={0} | all-to-all | bytes 524288 | tf_op jit(solution)/shard_map/all_to_all | solution.py:366
  97.7 0.7 reduce_sum.9
  (2 shorter events, 0.0 us)
Async XLA Ops:
  5.8 69.5 %all-to-all-start = ((f32[128,72,128]{2,1,0:T(8,128)}), f32[128,72,128]{2,1,0:T(8,128)}, u32[]{:S(2)}, u32[]{:S(2)}) async-start(f32[128,72,128]{2,1,0:T(8,128)} %pack.1), calls=%async_computation | async-start | bytes 9437184 | tf_op jit(solution)/shard_map/all_to_all | solution.py:360
  79.7 1.3 %collective-permute-start = (f32[8,8,128]{2,1,0:T(8,128)S(1)}, f32[8,8,128]{2,1,0:T(8,128)S(1)}, u32[]{:S(2)}, u32[]{:S(2)}) collective-permute-start(f32[8,8,128]{2,1,0:T(8,128)S(1)} %get-tuple-element.12), channel_id=1, source_target_pairs={{0,8},{8,0},{1,9},{9,1},{2,10},{10,2},{3,11},{11,3},{4,12},{12,4},... | collective-permute-start | bytes 98312 | tf_op jit(solution)/shard_map/ppermute | solution.py:363

commit v5 on v4

--- a/solution.py
+++ b/solution.py
@@ -15,7 +15,9 @@
 LANES = 128
 PACK_PEERS = 16
 PACK_GROUPS = DEVICES // PACK_PEERS
-PACK_ROWS = PACK_PEERS * WIDTH
+PACK_PAIRS = PACK_PEERS // 2
+PAIR_ROWS = 2 * WIDTH
+TILE = 8
 PEERS = 32
 GROUPS = DEVICES // PEERS
 LEFT_GROUPS = 20
@@ -48,25 +50,40 @@
 def pack_kernel(rank_ref, x_ref, v_ref, out_ref, rows_ref, own_ref, packed, in_sem, own_sem, out_sem):
     rank = rank_ref[0]
     own_group = rank // PACK_PEERS
-    first, last, whole = pl.ds(0, HALF), pl.ds(HALF, HALF), pl.ds(0, WIDTH)
-
-    def read(ref, columns, group):
-        source = ref.at[columns, pl.ds(group * PACK_ROWS, PACK_ROWS)]
-        return pltpu.make_async_copy(source, rows_ref.at[group, columns], in_sem.at[group])
-
-    def read_own():
-        source = v_ref.at[whole, pl.ds(own_group * PACK_ROWS, PACK_ROWS)]
-        return pltpu.make_async_copy(source, own_ref, own_sem)
-
-    def whole_rows(group, i, columns):
-        for n, c in enumerate(columns):
-            packed[group * PACK_PEERS + i, pl.ds(WIDTH * n, WIDTH), :] = rows_ref[group, c, pl.ds(WIDTH * i, WIDTH), :]
-
-    def half_rows(group, i, start):
+    own_half = HALF * (1 - lax.rem(rank, 2))
+
+    def whole_copies(ref, group):
+        columns = pl.ds(own_half, HALF)
+        source = ref.at[columns, pl.ds(group * PACK_PAIRS, PACK_PAIRS)]
+        return (pltpu.make_async_copy(source, rows_ref.at[group, pl.ds(0, HALF)], in_sem.at[group, 0]),)
+
+    def outer_copies(ref, group, target, sems):
+        pairs = pl.ds(group * PACK_PAIRS, PACK_PAIRS)
+        return tuple(
+            pltpu.make_async_copy(
+                ref.at[:, pairs, pl.ds(start, TILE)], target.at[:, :, pl.ds(start, TILE)], sems.at[n]
+            )
+            for n, start in enumerate((0, PAIR_ROWS - TILE))
+        )
+
+    def half_copies(ref, group):
+        return outer_copies(ref, group, rows_ref.at[group], in_sem.at[group])
+
+    def own_copies():
+        return outer_copies(v_ref, own_group, own_ref, own_sem)
+
+    def whole_rows(group, i):
+        for n in range(HALF):
+            rows = rows_ref[group, n, i // 2, pl.ds(WIDTH * (i % 2), WIDTH), :]
+            packed[group * PACK_PEERS + i, pl.ds(WIDTH * n, WIDTH), :] = rows
+
+    def half_start(i):
+        return (WIDTH + HALF) * (i % 2)
+
+    def half_rows(group, i):
         for c in range(WIDTH):
-            packed[group * PACK_PEERS + i, pl.ds(HALF * c, HALF), :] = rows_ref[
-                group, c, pl.ds(WIDTH * i + start, HALF), :
-            ]
+            rows = rows_ref[group, c, i // 2, pl.ds(half_start(i), HALF), :]
+            packed[group * PACK_PEERS + i, pl.ds(HALF * c, HALF), :] = rows
 
     def cases(group):
         above = group > own_group
@@ -74,51 +91,52 @@
         odd = lax.rem(group + own_group, 2) == 1
         even = jnp.logical_not(odd)
         return (
-            (jnp.logical_and(above, even), x_ref, first, lambda i: whole_rows(group, i, range(HALF))),
-            (jnp.logical_and(above, odd), x_ref, whole, lambda i: half_rows(group, i, 0)),
-            (jnp.logical_and(below, odd), v_ref, last, lambda i: whole_rows(group, i, range(HALF, WIDTH))),
-            (jnp.logical_and(below, even), v_ref, whole, lambda i: half_rows(group, i, HALF)),
+            (jnp.logical_and(above, even), x_ref, whole_copies, whole_rows),
+            (jnp.logical_and(above, odd), x_ref, half_copies, half_rows),
+            (jnp.logical_and(below, odd), v_ref, whole_copies, whole_rows),
+            (jnp.logical_and(below, even), v_ref, half_copies, half_rows),
         )
 
-    read(x_ref, first, own_group).start()
-    read_own().start()
+    for copy in whole_copies(x_ref, own_group) + own_copies():
+        copy.start()
     for group in range(PACK_GROUPS):
-        for condition, ref, columns, _ in cases(group):
+        for condition, ref, copies, _ in cases(group):
 
             @pl.when(condition)
             def _():
-                read(ref, columns, group).start()
+                for copy in copies(ref, group):
+                    copy.start()
 
     def write(group):
         peers = pl.ds(group * PACK_PEERS, PACK_PEERS)
         pltpu.make_async_copy(packed.at[peers], out_ref.at[peers], out_sem).start()
 
-    read(x_ref, first, own_group).wait()
-    read_own().wait()
+    for copy in whole_copies(x_ref, own_group) + own_copies():
+        copy.wait()
     for i in range(PACK_PEERS):
         below = own_group * PACK_PEERS + i < rank
 
         @pl.when(below)
         def _():
             for d in range(WIDTH):
-                packed[own_group * PACK_PEERS + i, pl.ds(HALF * d, HALF), :] = own_ref[
-                    d, pl.ds(WIDTH * i + HALF, HALF), :
-                ]
+                rows = own_ref[d, i // 2, pl.ds(half_start(i), HALF), :]
+                packed[own_group * PACK_PEERS + i, pl.ds(HALF * d, HALF), :] = rows
 
         @pl.when(jnp.logical_not(below))
         def _():
-            whole_rows(own_group, i, range(HALF))
+            whole_rows(own_group, i)
 
     write(own_group)
 
     def step(group, _):
-        for condition, ref, columns, move in cases(group):
+        for condition, ref, copies, move in cases(group):
 
             @pl.when(condition)
             def _():
-                read(ref, columns, group).wait()
+                for copy in copies(ref, group):
+                    copy.wait()
                 for i in range(PACK_PEERS):
-                    move(i)
+                    move(group, i)
                 write(group)
 
         return 0
@@ -128,6 +146,7 @@
 
 
 def pack(rank, x, v):
+    x, v = (array.reshape(WIDTH, DEVICES // 2, PAIR_ROWS, LANES) for array in (x, v))
     return pl.pallas_call(
         pack_kernel,
         in_specs=[
@@ -138,11 +157,11 @@
         out_specs=pl.BlockSpec(memory_space=pl.ANY),
         out_shape=jax.ShapeDtypeStruct((DEVICES, BLOCK, LANES), jnp.float32),
         scratch_shapes=[
-            pltpu.VMEM((PACK_GROUPS, WIDTH, PACK_ROWS, LANES), jnp.float32),
-            pltpu.VMEM((WIDTH, PACK_ROWS, LANES), jnp.float32),
+            pltpu.VMEM((PACK_GROUPS, WIDTH, PACK_PAIRS, PAIR_ROWS, LANES), jnp.float32),
+            pltpu.VMEM((WIDTH, PACK_PAIRS, PAIR_ROWS, LANES), jnp.float32),
             pltpu.VMEM((DEVICES, BLOCK, LANES), jnp.float32),
-            pltpu.SemaphoreType.DMA((PACK_GROUPS,)),
-            pltpu.SemaphoreType.DMA,
+            pltpu.SemaphoreType.DMA((PACK_GROUPS, 2)),
+            pltpu.SemaphoreType.DMA((2,)),
             pltpu.SemaphoreType.DMA,
         ],
         compiler_params=pltpu.CompilerParams(vmem_limit_bytes=VMEM_LIMIT),
@@ -161,6 +180,7 @@
         acc_ref[...] = jnp.zeros_like(acc_ref)
 
     own_pack_group = rank // PACK_PEERS
+    own_half = HALF * lax.rem(rank, 2)
     for i in range(PEERS):
         peer = group * PEERS + i
         odd = lax.rem(group * (PEERS // PACK_PEERS) + i // PACK_PEERS + own_pack_group, 2) == 1
@@ -168,25 +188,31 @@
         above = peer > rank
         below = peer < rank
 
+        def from_whole(ref):
+            start = WIDTH * i + HALF * (1 - i % 2)
+            for m in range(WIDTH):
+                terms_ref[pl.ds(BLOCK * i + m, HALF, stride=WIDTH), :] = ref[m, pl.ds(start, HALF), :]
+
+        def from_half(ref):
+            for m in range(HALF):
+                rows = ref[own_half + m, pl.ds(WIDTH * i, WIDTH), :]
+                terms_ref[pl.ds(BLOCK * i + m, WIDTH, stride=HALF), :] = rows
+
         @pl.when(jnp.logical_and(above, even))
         def _():
-            for c in range(HALF):
-                terms_ref[pl.ds(BLOCK * i + c, WIDTH, stride=HALF), :] = x_ref[HALF + c, pl.ds(WIDTH * i, WIDTH), :]
+            from_half(x_ref)
 
         @pl.when(jnp.logical_and(above, odd))
         def _():
-            for c in range(WIDTH):
-                terms_ref[pl.ds(BLOCK * i + c, HALF, stride=WIDTH), :] = x_ref[c, pl.ds(WIDTH * i + HALF, HALF), :]
+            from_whole(x_ref)
 
         @pl.when(jnp.logical_and(below, even))
         def _():
-            for d in range(WIDTH):
-                terms_ref[pl.ds(BLOCK * i + d, HALF, stride=WIDTH), :] = v_ref[d, pl.ds(WIDTH * i, HALF), :]
+            from_whole(v_ref)
 
         @pl.when(jnp.logical_and(below, odd))
         def _():
-            for d in range(HALF):
-                terms_ref[pl.ds(BLOCK * i + d, WIDTH, stride=HALF), :] = v_ref[d, pl.ds(WIDTH * i, WIDTH), :]
+            from_half(v_ref)
 
         @pl.when(peer == rank)
         def _():

time: 98.6 us -> 97.8 us (level)
  no operation moved by 1% of the time
where the time goes in v5:
time: 97.8 us; the launch traced here: 97.5 us
  waiting for transfers between devices  48.2 us (49%)
  Pallas kernels  20.3 us (21%)
  blocking collectives  16.6 us (17%)
  starting transfers between devices  11.7 us (12%)
    all_to_all x1, waiting for transfers between devices, body(): received = lax.all_to_all(pack(rank, x, v), AXES, 0, 0, tiled=True)  47 us
    all_to_all x1, blocking collectives, body(): return jnp.sum(lax.all_to_all(parts, CHIPS, 0, 0, tiled=True), axis=0)  16.6 us
    all_to_all x1, starting transfers between devices, body(): received = lax.all_to_all(pack(rank, x, v), AXES, 0, 0, tiled=True)  11.6 us
    pallas_call x1, Pallas kernels, local(): pl.pallas_call(local_kernel, grid_spec=pltpu.PrefetchScalarGridSpec(num_s...  10.8 us
    pallas_call x1, Pallas kernels, pack(): pl.pallas_call(pack_kernel, in_specs=[pl.BlockSpec(memory_space=pltpu.SME...  4.98 us
    pallas_call x1, Pallas kernels, mirror(): pl.pallas_call(mirror_kernel, in_specs=[pl.BlockSpec(memory_space=pltpu.S...  4.47 us
  transfers between devices with their start and end apart: 2, of which 2 were waited for; matrix products, arithmetic and copies ran while one was open for 0% of the time, Pallas kernels for 11%

profile of v5, /device:TPU:0, one launch (start us, length us, event | category | flops | bytes accessed | tf_op | source)
XLA Modules:
  0.0 97.5 jit_solution(10101918892958423847)
XLA Ops:
  0.0 5.0 %pack.1 = f32[128,72,128]{2,1,0:T(8,128)} custom-call(s32[1]{0:T(128)} %bitcast.rank_ref, f32[12,64,24,128]{3,2,1,0:T(8,128)} %bitcast.8, f32[12,64,24,128]{3,2,1,0:T(8,128)} %bitcast.10), custom_call_target="tpu_custom_call" | custom-call | bytes 12000000 | tf_op jit(solution)/shard_map/pack/pallas_call | solution.py:150
  5.0 11.6 %all-to-all-start = ((f32[128,72,128]{2,1,0:T(8,128)}), f32[128,72,128]{2,1,0:T(8,128)}, u32[]{:S(2)}, u32[]{:S(2)}) async-start(f32[128,72,128]{2,1,0:T(8,128)} %pack.1), calls=%async_computation | async-start | bytes 9437184 | tf_op jit(solution)/shard_map/all_to_all | solution.py:386
  16.6 10.8 %local.1 = (bf16[20,256,2304]{2,1,0:T(8,128)(2,1)}, f32[320,128,128]{2,1,0:T(8,128)}) custom-call(s32[1]{0:T(128)} %bitcast.rank_ref, f32[12,1536,128]{2,1,0:T(8,128)} %bitcast.9, f32[12,1536,128]{2,1,0:T(8,128)} %bitcast.11), custom_call_target="tpu_custom_call" | custom-call | flops 20000000000 | bytes 30000000 | tf_op jit(solution)/shard_map/local/pallas_call | solution.py:253
  27.4 47.0 %all-to-all-done.received_ref = f32[128,72,128]{2,1,0:T(8,128)} async-done(((f32[128,72,128]{2,1,0:T(8,128)}), f32[128,72,128]{2,1,0:T(8,128)}, u32[]{:S(2)}, u32[]{:S(2)}) %all-to-all-start) | async-done | bytes 4718624 | tf_op jit(solution)/shard_map/all_to_all | solution.py:386
  74.4 4.5 %mirror.1 = (f32[8,8,128]{2,1,0:T(8,128)S(1)}, f32[8,8,128]{2,1,0:T(8,128)S(1)}) custom-call(s32[1]{0:T(128)} %bitcast.rank_ref, bf16[20,256,2304]{2,1,0:T(8,128)(2,1)} %get-tuple-element.9.left_ref, f32[128,72,128]{2,1,0:T(8,128)} %all-to-all-done.received_ref, f32[320,128,128]{2,1,0:T(8,128)} %get-tuple-element.10.direct_ref), custom_call_target="tpu_custom_call" | custom-call | flops 2500000000 | bytes 10000000 | tf_op jit(solution)/shard_map/mirror/pallas_call | solution.py:356
  78.9 0.1 collective-permute-start
  79.0 1.2 %collective-permute-done = f32[8,8,128]{2,1,0:T(8,128)S(1)} collective-permute-done((f32[8,8,128]{2,1,0:T(8,128)S(1)}, f32[8,8,128]{2,1,0:T(8,128)S(1)}, u32[]{:S(2)}, u32[]{:S(2)}) %collective-permute-start) | collective-permute-done | bytes 32800 | tf_op jit(solution)/shard_map/ppermute | solution.py:389
  80.2 16.6 %all_to_all.10 = f32[64,8,128]{2,1,0:T(8,128)S(1)} all-to-all(f32[64,8,128]{2,1,0:T(8,128)S(1)} %bitcast.12), channel_id=1, replica_groups=mesh['half'=8,'core'=2,'col'=8] {'half','col'}, dimensions={0} | all-to-all | bytes 524288 | tf_op jit(solution)/shard_map/all_to_all | solution.py:392
  96.8 0.7 reduce_sum.9
  (2 shorter events, 0.0 us)
Async XLA Ops:
  5.0 69.4 %all-to-all-start = ((f32[128,72,128]{2,1,0:T(8,128)}), f32[128,72,128]{2,1,0:T(8,128)}, u32[]{:S(2)}, u32[]{:S(2)}) async-start(f32[128,72,128]{2,1,0:T(8,128)} %pack.1), calls=%async_computation | async-start | bytes 9437184 | tf_op jit(solution)/shard_map/all_to_all | solution.py:386
  78.9 1.3 %collective-permute-start = (f32[8,8,128]{2,1,0:T(8,128)S(1)}, f32[8,8,128]{2,1,0:T(8,128)S(1)}, u32[]{:S(2)}, u32[]{:S(2)}) collective-permute-start(f32[8,8,128]{2,1,0:T(8,128)S(1)} %get-tuple-element.12), channel_id=1, source_target_pairs={{0,8},{8,0},{1,9},{9,1},{2,10},{10,2},{3,11},{11,3},{4,12},{12,4},... | collective-permute-start | bytes 98312 | tf_op jit(solution)/shard_map/ppermute | solution.py:389

commit v6 on v5

--- a/solution.py
+++ b/solution.py
@@ -52,92 +52,84 @@
     own_group = rank // PACK_PEERS
     own_half = HALF * (1 - lax.rem(rank, 2))
 
-    def whole_copies(ref, group):
-        columns = pl.ds(own_half, HALF)
-        source = ref.at[columns, pl.ds(group * PACK_PAIRS, PACK_PAIRS)]
-        return (pltpu.make_async_copy(source, rows_ref.at[group, pl.ds(0, HALF)], in_sem.at[group, 0]),)
-
-    def outer_copies(ref, group, target, sems):
+    def v_copies(group, target, sem):
+        source = v_ref.at[pl.ds(own_half, HALF), pl.ds(group * PACK_PAIRS, PACK_PAIRS)]
+        return (pltpu.make_async_copy(source, target, sem),)
+
+    def x_copies(group):
         pairs = pl.ds(group * PACK_PAIRS, PACK_PAIRS)
         return tuple(
             pltpu.make_async_copy(
-                ref.at[:, pairs, pl.ds(start, TILE)], target.at[:, :, pl.ds(start, TILE)], sems.at[n]
+                x_ref.at[:, pairs, pl.ds(start, TILE)], rows_ref.at[group, :, :, pl.ds(start, TILE)], in_sem.at[group, n]
             )
             for n, start in enumerate((0, PAIR_ROWS - TILE))
         )
 
-    def half_copies(ref, group):
-        return outer_copies(ref, group, rows_ref.at[group], in_sem.at[group])
+    def below_copies(group):
+        return v_copies(group, rows_ref.at[group, pl.ds(0, HALF)], in_sem.at[group, 0])
 
     def own_copies():
-        return outer_copies(v_ref, own_group, own_ref, own_sem)
-
-    def whole_rows(group, i):
+        return x_copies(own_group) + v_copies(own_group, own_ref, own_sem)
+
+    def pack_v(group, i, source):
         for n in range(HALF):
-            rows = rows_ref[group, n, i // 2, pl.ds(WIDTH * (i % 2), WIDTH), :]
+            rows = source[n, i // 2, pl.ds(WIDTH * (i % 2), WIDTH), :]
             packed[group * PACK_PEERS + i, pl.ds(WIDTH * n, WIDTH), :] = rows
 
-    def half_start(i):
-        return (WIDTH + HALF) * (i % 2)
-
-    def half_rows(group, i):
+    def pack_x(group, i):
         for c in range(WIDTH):
-            rows = rows_ref[group, c, i // 2, pl.ds(half_start(i), HALF), :]
+            rows = rows_ref[group, c, i // 2, pl.ds((WIDTH + HALF) * (i % 2), HALF), :]
             packed[group * PACK_PEERS + i, pl.ds(HALF * c, HALF), :] = rows
 
-    def cases(group):
-        above = group > own_group
-        below = group < own_group
-        odd = lax.rem(group + own_group, 2) == 1
-        even = jnp.logical_not(odd)
-        return (
-            (jnp.logical_and(above, even), x_ref, whole_copies, whole_rows),
-            (jnp.logical_and(above, odd), x_ref, half_copies, half_rows),
-            (jnp.logical_and(below, odd), v_ref, whole_copies, whole_rows),
-            (jnp.logical_and(below, even), v_ref, half_copies, half_rows),
-        )
-
-    for copy in whole_copies(x_ref, own_group) + own_copies():
+    for copy in own_copies():
         copy.start()
     for group in range(PACK_GROUPS):
-        for condition, ref, copies, _ in cases(group):
-
-            @pl.when(condition)
-            def _():
-                for copy in copies(ref, group):
-                    copy.start()
+
+        @pl.when(group > own_group)
+        def _():
+            for copy in x_copies(group):
+                copy.start()
+
+        @pl.when(group < own_group)
+        def _():
+            for copy in below_copies(group):
+                copy.start()
 
     def write(group):
         peers = pl.ds(group * PACK_PEERS, PACK_PEERS)
         pltpu.make_async_copy(packed.at[peers], out_ref.at[peers], out_sem).start()
 
-    for copy in whole_copies(x_ref, own_group) + own_copies():
+    for copy in own_copies():
         copy.wait()
     for i in range(PACK_PEERS):
         below = own_group * PACK_PEERS + i < rank
 
         @pl.when(below)
         def _():
-            for d in range(WIDTH):
-                rows = own_ref[d, i // 2, pl.ds(half_start(i), HALF), :]
-                packed[own_group * PACK_PEERS + i, pl.ds(HALF * d, HALF), :] = rows
+            pack_v(own_group, i, own_ref)
 
         @pl.when(jnp.logical_not(below))
         def _():
-            whole_rows(own_group, i)
+            pack_x(own_group, i)
 
     write(own_group)
 
     def step(group, _):
-        for condition, ref, copies, move in cases(group):
-
-            @pl.when(condition)
-            def _():
-                for copy in copies(ref, group):
-                    copy.wait()
-                for i in range(PACK_PEERS):
-                    move(group, i)
-                write(group)
+        @pl.when(group > own_group)
+        def _():
+            for copy in x_copies(group):
+                copy.wait()
+            for i in range(PACK_PEERS):
+                pack_x(group, i)
+            write(group)
+
+        @pl.when(group < own_group)
+        def _():
+            for copy in below_copies(group):
+                copy.wait()
+            for i in range(PACK_PEERS):
+                pack_v(group, i, rows_ref.at[group])
+            write(group)
 
         return 0
 
@@ -158,10 +150,10 @@
         out_shape=jax.ShapeDtypeStruct((DEVICES, BLOCK, LANES), jnp.float32),
         scratch_shapes=[
             pltpu.VMEM((PACK_GROUPS, WIDTH, PACK_PAIRS, PAIR_ROWS, LANES), jnp.float32),
-            pltpu.VMEM((WIDTH, PACK_PAIRS, PAIR_ROWS, LANES), jnp.float32),
+            pltpu.VMEM((HALF, PACK_PAIRS, PAIR_ROWS, LANES), jnp.float32),
             pltpu.VMEM((DEVICES, BLOCK, LANES), jnp.float32),
             pltpu.SemaphoreType.DMA((PACK_GROUPS, 2)),
-            pltpu.SemaphoreType.DMA((2,)),
+            pltpu.SemaphoreType.DMA,
             pltpu.SemaphoreType.DMA,
         ],
         compiler_params=pltpu.CompilerParams(vmem_limit_bytes=VMEM_LIMIT),
@@ -179,40 +171,21 @@
     def _():
         acc_ref[...] = jnp.zeros_like(acc_ref)
 
-    own_pack_group = rank // PACK_PEERS
     own_half = HALF * lax.rem(rank, 2)
     for i in range(PEERS):
         peer = group * PEERS + i
-        odd = lax.rem(group * (PEERS // PACK_PEERS) + i // PACK_PEERS + own_pack_group, 2) == 1
-        even = jnp.logical_not(odd)
-        above = peer > rank
-        below = peer < rank
-
-        def from_whole(ref):
+
+        @pl.when(peer > rank)
+        def _():
             start = WIDTH * i + HALF * (1 - i % 2)
             for m in range(WIDTH):
-                terms_ref[pl.ds(BLOCK * i + m, HALF, stride=WIDTH), :] = ref[m, pl.ds(start, HALF), :]
-
-        def from_half(ref):
+                terms_ref[pl.ds(BLOCK * i + m, HALF, stride=WIDTH), :] = x_ref[m, pl.ds(start, HALF), :]
+
+        @pl.when(peer < rank)
+        def _():
             for m in range(HALF):
-                rows = ref[own_half + m, pl.ds(WIDTH * i, WIDTH), :]
+                rows = v_ref[own_half + m, pl.ds(WIDTH * i, WIDTH), :]
                 terms_ref[pl.ds(BLOCK * i + m, WIDTH, stride=HALF), :] = rows
-
-        @pl.when(jnp.logical_and(above, even))
-        def _():
-            from_half(x_ref)
-
-        @pl.when(jnp.logical_and(above, odd))
-        def _():
-            from_whole(x_ref)
-
-        @pl.when(jnp.logical_and(below, even))
-        def _():
-            from_whole(v_ref)
-
-        @pl.when(jnp.logical_and(below, odd))
-        def _():
-            from_half(v_ref)
 
         @pl.when(peer == rank)
         def _():

time: 97.8 us -> 97 us (level)
  starting transfers between devices: 11.7 us -> 10.5 us
    all_to_all x1, starting transfers between devices: 11.6 us -> 10.4 us  [body(): received = lax.all_to_all(pack(rank, x, v), AXES, 0, 0, tiled=True)]
  transfers between devices with their start and end apart: 2 -> 2, of which waited for: 2 -> 2; matrix products, arithmetic and copies ran while one was open for 0% -> 0% of each run, Pallas kernels for 11% -> 10%
where the time goes in v6:
time: 97 us; the launch traced here: 96.7 us
  waiting for transfers between devices  49.1 us (51%)
  Pallas kernels  19.7 us (20%)
  blocking collectives  16.6 us (17%)
  starting transfers between devices  10.5 us (11%)
    all_to_all x1, waiting for transfers between devices, body(): received = lax.all_to_all(pack(rank, x, v), AXES, 0, 0, tiled=True)  47.9 us
    all_to_all x1, blocking collectives, body(): return jnp.sum(lax.all_to_all(parts, CHIPS, 0, 0, tiled=True), axis=0)  16.6 us
    all_to_all x1, starting transfers between devices, body(): received = lax.all_to_all(pack(rank, x, v), AXES, 0, 0, tiled=True)  10.4 us
    pallas_call x1, Pallas kernels, local(): pl.pallas_call(local_kernel, grid_spec=pltpu.PrefetchScalarGridSpec(num_s...  9.92 us
    pallas_call x1, Pallas kernels, pack(): pl.pallas_call(pack_kernel, in_specs=[pl.BlockSpec(memory_space=pltpu.SME...  5.34 us
    pallas_call x1, Pallas kernels, mirror(): pl.pallas_call(mirror_kernel, in_specs=[pl.BlockSpec(memory_space=pltpu.S...  4.47 us
  transfers between devices with their start and end apart: 2, of which 2 were waited for; matrix products, arithmetic and copies ran while one was open for 0% of the time, Pallas kernels for 10%

profile of v6, /device:TPU:0, one launch (start us, length us, event | category | flops | bytes accessed | tf_op | source)
XLA Modules:
  0.0 96.7 jit_solution(1295012054758705471)
XLA Ops:
  0.0 5.3 %pack.1 = f32[128,72,128]{2,1,0:T(8,128)} custom-call(s32[1]{0:T(128)} %bitcast.rank_ref, f32[12,64,24,128]{3,2,1,0:T(8,128)} %bitcast.8, f32[12,64,24,128]{3,2,1,0:T(8,128)} %bitcast.10), custom_call_target="tpu_custom_call" | custom-call | bytes 12000000 | tf_op jit(solution)/shard_map/pack/pallas_call | solution.py:142
  5.4 10.4 %all-to-all-start = ((f32[128,72,128]{2,1,0:T(8,128)}), f32[128,72,128]{2,1,0:T(8,128)}, u32[]{:S(2)}, u32[]{:S(2)}) async-start(f32[128,72,128]{2,1,0:T(8,128)} %pack.1), calls=%async_computation | async-start | bytes 9437184 | tf_op jit(solution)/shard_map/all_to_all | solution.py:359
  15.8 9.9 %local.1 = (bf16[20,256,2304]{2,1,0:T(8,128)(2,1)}, f32[320,128,128]{2,1,0:T(8,128)}) custom-call(s32[1]{0:T(128)} %bitcast.rank_ref, f32[12,1536,128]{2,1,0:T(8,128)} %bitcast.9, f32[12,1536,128]{2,1,0:T(8,128)} %bitcast.11), custom_call_target="tpu_custom_call" | custom-call | flops 20000000000 | bytes 30000000 | tf_op jit(solution)/shard_map/local/pallas_call | solution.py:226
  25.7 47.9 %all-to-all-done.received_ref = f32[128,72,128]{2,1,0:T(8,128)} async-done(((f32[128,72,128]{2,1,0:T(8,128)}), f32[128,72,128]{2,1,0:T(8,128)}, u32[]{:S(2)}, u32[]{:S(2)}) %all-to-all-start) | async-done | bytes 4718624 | tf_op jit(solution)/shard_map/all_to_all | solution.py:359
  73.6 4.5 %mirror.1 = (f32[8,8,128]{2,1,0:T(8,128)S(1)}, f32[8,8,128]{2,1,0:T(8,128)S(1)}) custom-call(s32[1]{0:T(128)} %bitcast.rank_ref, bf16[20,256,2304]{2,1,0:T(8,128)(2,1)} %get-tuple-element.9.left_ref, f32[128,72,128]{2,1,0:T(8,128)} %all-to-all-done.received_ref, f32[320,128,128]{2,1,0:T(8,128)} %get-tuple-element.10.direct_ref), custom_call_target="tpu_custom_call" | custom-call | flops 2500000000 | bytes 10000000 | tf_op jit(solution)/shard_map/mirror/pallas_call | solution.py:329
  78.1 0.1 collective-permute-start
  78.2 1.2 %collective-permute-done = f32[8,8,128]{2,1,0:T(8,128)S(1)} collective-permute-done((f32[8,8,128]{2,1,0:T(8,128)S(1)}, f32[8,8,128]{2,1,0:T(8,128)S(1)}, u32[]{:S(2)}, u32[]{:S(2)}) %collective-permute-start) | collective-permute-done | bytes 32800 | tf_op jit(solution)/shard_map/ppermute | solution.py:362
  79.4 16.6 %all_to_all.10 = f32[64,8,128]{2,1,0:T(8,128)S(1)} all-to-all(f32[64,8,128]{2,1,0:T(8,128)S(1)} %bitcast.12), channel_id=1, replica_groups=mesh['half'=8,'core'=2,'col'=8] {'half','col'}, dimensions={0} | all-to-all | bytes 524288 | tf_op jit(solution)/shard_map/all_to_all | solution.py:365
  96.1 0.7 reduce_sum.9
  (2 shorter events, 0.0 us)
Async XLA Ops:
  5.4 68.3 %all-to-all-start = ((f32[128,72,128]{2,1,0:T(8,128)}), f32[128,72,128]{2,1,0:T(8,128)}, u32[]{:S(2)}, u32[]{:S(2)}) async-start(f32[128,72,128]{2,1,0:T(8,128)} %pack.1), calls=%async_computation | async-start | bytes 9437184 | tf_op jit(solution)/shard_map/all_to_all | solution.py:359
  78.1 1.3 %collective-permute-start = (f32[8,8,128]{2,1,0:T(8,128)S(1)}, f32[8,8,128]{2,1,0:T(8,128)S(1)}, u32[]{:S(2)}, u32[]{:S(2)}) collective-permute-start(f32[8,8,128]{2,1,0:T(8,128)S(1)} %get-tuple-element.12), channel_id=1, source_target_pairs={{0,8},{8,0},{1,9},{9,1},{2,10},{10,2},{3,11},{11,3},{4,12},{12,4},... | collective-permute-start | bytes 98312 | tf_op jit(solution)/shard_map/ppermute | solution.py:362

commit v7 on v6

--- a/solution.py
+++ b/solution.py
@@ -20,6 +20,7 @@
 TILE = 8
 PEERS = 32
 GROUPS = DEVICES // PEERS
+PIECES = ((0, 1536), (1536, 768))
 LEFT_GROUPS = 20
 DIRECT_LENGTH = 320
 ROWS = PEERS * WIDTH
@@ -272,16 +273,26 @@
     rank = rank_ref[0]
     own_group = rank // PEERS
 
-    def copies(turn):
+    last = GROUPS - 1
+
+    def copies(turn, start=0, length=TERMS, sem=None):
         group = lax.rem(own_group + turn, GROUPS)
-        peers = pl.ds(group * PEERS, PEERS)
+        sem = turn if sem is None else sem
+        terms = pl.ds(start, length)
+        rows = received_ref.at[pl.ds(group * TERMS + start, length)]
         return (
-            pltpu.make_async_copy(received_ref.at[peers], received.at[turn], received_sem.at[turn]),
-            pltpu.make_async_copy(left_ref.at[group], left.at[turn], left_sem.at[turn]),
+            pltpu.make_async_copy(rows, received.at[turn, terms], received_sem.at[sem]),
+            pltpu.make_async_copy(left_ref.at[group, :, terms], left.at[turn, :, terms], left_sem.at[sem]),
         )
 
-    for turn in range(GROUPS):
+    def last_copies(piece):
+        return copies(last, *PIECES[piece], last + piece)
+
+    for turn in range(last):
         for copy in copies(turn):
+            copy.start()
+    for piece in range(len(PIECES)):
+        for copy in last_copies(piece):
             copy.start()
     direct_copy = pltpu.make_async_copy(direct_ref.at[0], direct, direct_sem)
     direct_copy.start()
@@ -291,7 +302,7 @@
 
     for copy in copies(0):
         copy.wait()
-    values = received[0].reshape(TERMS, LANES)
+    values = received[0]
     term = lax.broadcasted_iota(jnp.int32, (TERMS, LANES), 0)
     first = (rank - own_group * PEERS) * BLOCK
     below_ref[...] = product(0, jnp.where(term < first, values, 0.0))
@@ -300,7 +311,7 @@
     def step(turn, _):
         for copy in copies(turn):
             copy.wait()
-        values = received[turn].reshape(TERMS, LANES)
+        values = received[turn]
         below = own_group + turn >= GROUPS
 
         @pl.when(below)
@@ -313,7 +324,23 @@
 
         return 0
 
-    lax.fori_loop(1, GROUPS, step, 0)
+    lax.fori_loop(1, last, step, 0)
+    for piece, (start, length) in enumerate(PIECES):
+        for copy in last_copies(piece):
+            copy.wait()
+        terms = pl.ds(start, length)
+        right = jnp.concatenate(split(received[last, terms]), axis=1)
+        part = dot(left[last, :, terms], right)
+        below = own_group + last >= GROUPS
+
+        @pl.when(below)
+        def _():
+            below_ref[...] += part
+
+        @pl.when(jnp.logical_not(below))
+        def _():
+            above_ref[...] += part
+
     direct_copy.wait()
     total = direct[...] - (fold(above_ref[...]) + fold(below_ref[...]).T)
     first_core = lax.rem(rank // COL_DEVICES, CORES) == 0
@@ -338,18 +365,18 @@
         out_shape=[jax.ShapeDtypeStruct((HALVES, OUT_ROWS, LANES), jnp.float32)] * 2,
         scratch_shapes=[
             pltpu.VMEM((GROUPS, 2 * LANES, TERMS), jnp.bfloat16),
-            pltpu.VMEM((GROUPS, PEERS, BLOCK, LANES), jnp.float32),
+            pltpu.VMEM((GROUPS, TERMS, LANES), jnp.float32),
             pltpu.VMEM((LANES, LANES), jnp.float32),
             pltpu.VMEM((2 * LANES, 2 * LANES), jnp.float32),
             pltpu.VMEM((2 * LANES, 2 * LANES), jnp.float32),
-            pltpu.SemaphoreType.DMA((GROUPS,)),
-            pltpu.SemaphoreType.DMA((GROUPS,)),
+            pltpu.SemaphoreType.DMA((GROUPS - 1 + len(PIECES),)),
+            pltpu.SemaphoreType.DMA((GROUPS - 1 + len(PIECES),)),
             pltpu.SemaphoreType.DMA,
         ],
         compiler_params=pltpu.CompilerParams(vmem_limit_bytes=MIRROR_VMEM_LIMIT),
         cost_estimate=pl.CostEstimate(flops=2_500_000_000, bytes_accessed=10_000_000, transcendentals=0),
         name="mirror",
-    )(rank, left, received, direct)
+    )(rank, left, received.reshape(DEVICES * BLOCK, LANES), direct)
 
 
 def body(cycle_inter, integrals):

time: 97 us -> 97.2 us (level)
  no operation moved by 1% of the time
where the time goes in v7:
time: 97.2 us; the launch traced here: 96.9 us
  waiting for transfers between devices  49.1 us (51%)
  Pallas kernels  19.9 us (20%)
  blocking collectives  16.6 us (17%)
  starting transfers between devices  10.5 us (11%)
    all_to_all x1, waiting for transfers between devices, body(): received = lax.all_to_all(pack(rank, x, v), AXES, 0, 0, tiled=True)  47.9 us
    all_to_all x1, blocking collectives, body(): return jnp.sum(lax.all_to_all(parts, CHIPS, 0, 0, tiled=True), axis=0)  16.6 us
    all_to_all x1, starting transfers between devices, body(): received = lax.all_to_all(pack(rank, x, v), AXES, 0, 0, tiled=True)  10.4 us
    pallas_call x1, Pallas kernels, local(): pl.pallas_call(local_kernel, grid_spec=pltpu.PrefetchScalarGridSpec(num_s...  9.92 us
    pallas_call x1, Pallas kernels, pack(): pl.pallas_call(pack_kernel, in_specs=[pl.BlockSpec(memory_space=pltpu.SME...  5.34 us
    pallas_call x1, Pallas kernels, mirror(): pl.pallas_call(mirror_kernel, in_specs=[pl.BlockSpec(memory_space=pltpu.S...  4.68 us
  transfers between devices with their start and end apart: 2, of which 2 were waited for; matrix products, arithmetic and copies ran while one was open for 0% of the time, Pallas kernels for 10%

profile of v7, /device:TPU:0, one launch (start us, length us, event | category | flops | bytes accessed | tf_op | source)
XLA Modules:
  0.0 96.9 jit_solution(18243156439379091610)
XLA Ops:
  0.0 5.3 %pack.1 = f32[128,72,128]{2,1,0:T(8,128)} custom-call(s32[1]{0:T(128)} %bitcast.rank_ref, f32[12,64,24,128]{3,2,1,0:T(8,128)} %bitcast.9, f32[12,64,24,128]{3,2,1,0:T(8,128)} %bitcast.11), custom_call_target="tpu_custom_call" | custom-call | bytes 12000000 | tf_op jit(solution)/shard_map/pack/pallas_call | solution.py:143
  5.4 10.4 %all-to-all-start = ((f32[128,72,128]{2,1,0:T(8,128)}), f32[128,72,128]{2,1,0:T(8,128)}, u32[]{:S(2)}, u32[]{:S(2)}) async-start(f32[128,72,128]{2,1,0:T(8,128)} %pack.1), calls=%async_computation | async-start | bytes 9437184 | tf_op jit(solution)/shard_map/all_to_all | solution.py:386
  15.8 9.9 %local.1 = (bf16[20,256,2304]{2,1,0:T(8,128)(2,1)}, f32[320,128,128]{2,1,0:T(8,128)}) custom-call(s32[1]{0:T(128)} %bitcast.rank_ref, f32[12,1536,128]{2,1,0:T(8,128)} %bitcast.10, f32[12,1536,128]{2,1,0:T(8,128)} %bitcast.12), custom_call_target="tpu_custom_call" | custom-call | flops 20000000000 | bytes 30000000 | tf_op jit(solution)/shard_map/local/pallas_call | solution.py:227
  25.7 47.9 %all-to-all-done = f32[128,72,128]{2,1,0:T(8,128)} async-done(((f32[128,72,128]{2,1,0:T(8,128)}), f32[128,72,128]{2,1,0:T(8,128)}, u32[]{:S(2)}, u32[]{:S(2)}) %all-to-all-start) | async-done | bytes 4718624 | tf_op jit(solution)/shard_map/all_to_all | solution.py:386
  73.6 4.7 %mirror.1 = (f32[8,8,128]{2,1,0:T(8,128)S(1)}, f32[8,8,128]{2,1,0:T(8,128)S(1)}) custom-call(s32[1]{0:T(128)} %bitcast.rank_ref, bf16[20,256,2304]{2,1,0:T(8,128)(2,1)} %get-tuple-element.9.left_ref, f32[9216,128]{1,0:T(8,128)} %bitcast.5.received_ref, f32[320,128,128]{2,1,0:T(8,128)} %get-tuple-element.10.direct_ref), custom_call_target="tpu_custom_call" | custom-call | flops 2500000000 | bytes 10000000 | tf_op jit(solution)/shard_map/mirror/pallas_call | solution.py:356
  78.3 0.1 collective-permute-start
  78.4 1.2 %collective-permute-done = f32[8,8,128]{2,1,0:T(8,128)S(1)} collective-permute-done((f32[8,8,128]{2,1,0:T(8,128)S(1)}, f32[8,8,128]{2,1,0:T(8,128)S(1)}, u32[]{:S(2)}, u32[]{:S(2)}) %collective-permute-start) | collective-permute-done | bytes 32800 | tf_op jit(solution)/shard_map/ppermute | solution.py:389
  79.6 16.6 %all_to_all.10 = f32[64,8,128]{2,1,0:T(8,128)S(1)} all-to-all(f32[64,8,128]{2,1,0:T(8,128)S(1)} %bitcast.13), channel_id=1, replica_groups=mesh['half'=8,'core'=2,'col'=8] {'half','col'}, dimensions={0} | all-to-all | bytes 524288 | tf_op jit(solution)/shard_map/all_to_all | solution.py:392
  96.3 0.7 reduce_sum.9
  (2 shorter events, 0.0 us)
Async XLA Ops:
  5.4 68.3 %all-to-all-start = ((f32[128,72,128]{2,1,0:T(8,128)}), f32[128,72,128]{2,1,0:T(8,128)}, u32[]{:S(2)}, u32[]{:S(2)}) async-start(f32[128,72,128]{2,1,0:T(8,128)} %pack.1), calls=%async_computation | async-start | bytes 9437184 | tf_op jit(solution)/shard_map/all_to_all | solution.py:386
  78.3 1.3 %collective-permute-start = (f32[8,8,128]{2,1,0:T(8,128)S(1)}, f32[8,8,128]{2,1,0:T(8,128)S(1)}, u32[]{:S(2)}, u32[]{:S(2)}) collective-permute-start(f32[8,8,128]{2,1,0:T(8,128)S(1)} %get-tuple-element.12), channel_id=1, source_target_pairs={{0,8},{8,0},{1,9},{9,1},{2,10},{10,2},{3,11},{11,3},{4,12},{12,4},... | collective-permute-start | bytes 98312 | tf_op jit(solution)/shard_map/ppermute | solution.py:389

commit v8 on v6

--- a/solution.py
+++ b/solution.py
@@ -71,15 +71,23 @@
     def own_copies():
         return x_copies(own_group) + v_copies(own_group, own_ref, own_sem)
 
-    def pack_v(group, i, source):
+    def pack_v(group, pair, odd, source):
         for n in range(HALF):
-            rows = source[n, i // 2, pl.ds(WIDTH * (i % 2), WIDTH), :]
-            packed[group * PACK_PEERS + i, pl.ds(WIDTH * n, WIDTH), :] = rows
-
-    def pack_x(group, i):
+            rows = source[n, pair, pl.ds(WIDTH * odd, WIDTH), :]
+            packed[group * PACK_PEERS + 2 * pair + odd, pl.ds(WIDTH * n, WIDTH), :] = rows
+
+    def pack_x(group, pair, odd):
         for c in range(WIDTH):
-            rows = rows_ref[group, c, i // 2, pl.ds((WIDTH + HALF) * (i % 2), HALF), :]
-            packed[group * PACK_PEERS + i, pl.ds(HALF * c, HALF), :] = rows
+            rows = rows_ref[group, c, pair, pl.ds((WIDTH + HALF) * odd, HALF), :]
+            packed[group * PACK_PEERS + 2 * pair + odd, pl.ds(HALF * c, HALF), :] = rows
+
+    def over_peers(move):
+        def pair_step(pair, _):
+            for odd in range(2):
+                move(pair, odd)
+            return 0
+
+        lax.fori_loop(0, PACK_PAIRS, pair_step, 0)
 
     for copy in own_copies():
         copy.start()
@@ -101,17 +109,19 @@
 
     for copy in own_copies():
         copy.wait()
-    for i in range(PACK_PEERS):
-        below = own_group * PACK_PEERS + i < rank
+
+    def pack_own(pair, odd):
+        below = own_group * PACK_PEERS + 2 * pair + odd < rank
 
         @pl.when(below)
         def _():
-            pack_v(own_group, i, own_ref)
+            pack_v(own_group, pair, odd, own_ref)
 
         @pl.when(jnp.logical_not(below))
         def _():
-            pack_x(own_group, i)
-
+            pack_x(own_group, pair, odd)
+
+    over_peers(pack_own)
     write(own_group)
 
     def step(group, _):
@@ -119,16 +129,14 @@
         def _():
             for copy in x_copies(group):
                 copy.wait()
-            for i in range(PACK_PEERS):
-                pack_x(group, i)
+            over_peers(lambda pair, odd: pack_x(group, pair, odd))
             write(group)
 
         @pl.when(group < own_group)
         def _():
             for copy in below_copies(group):
                 copy.wait()
-            for i in range(PACK_PEERS):
-                pack_v(group, i, rows_ref.at[group])
+            over_peers(lambda pair, odd: pack_v(group, pair, odd, rows_ref.at[group]))
             write(group)
 
         return 0

time: 97 us -> 96.9 us (level)
  no operation moved by 1% of the time
where the time goes in v8:
time: 96.9 us; the launch traced here: 96.6 us
  waiting for transfers between devices  49.1 us (51%)
  Pallas kernels  19.8 us (20%)
  blocking collectives  16.6 us (17%)
  starting transfers between devices  10.4 us (11%)
    all_to_all x1, waiting for transfers between devices, body(): received = lax.all_to_all(pack(rank, x, v), AXES, 0, 0, tiled=True)  47.9 us
    all_to_all x1, blocking collectives, body(): return jnp.sum(lax.all_to_all(parts, CHIPS, 0, 0, tiled=True), axis=0)  16.6 us
    all_to_all x1, starting transfers between devices, body(): received = lax.all_to_all(pack(rank, x, v), AXES, 0, 0, tiled=True)  10.3 us
    pallas_call x1, Pallas kernels, local(): pl.pallas_call(local_kernel, grid_spec=pltpu.PrefetchScalarGridSpec(num_s...  9.91 us
    pallas_call x1, Pallas kernels, pack(): pl.pallas_call(pack_kernel, in_specs=[pl.BlockSpec(memory_space=pltpu.SME...  5.38 us
    pallas_call x1, Pallas kernels, mirror(): pl.pallas_call(mirror_kernel, in_specs=[pl.BlockSpec(memory_space=pltpu.S...  4.47 us
  transfers between devices with their start and end apart: 2, of which 2 were waited for; matrix products, arithmetic and copies ran while one was open for 0% of the time, Pallas kernels for 10%

profile of v8, /device:TPU:0, one launch (start us, length us, event | category | flops | bytes accessed | tf_op | source)
XLA Modules:
  0.0 96.6 jit_solution(17899850036689600791)
XLA Ops:
  0.0 5.4 %pack.1 = f32[128,72,128]{2,1,0:T(8,128)} custom-call(s32[1]{0:T(128)} %bitcast.rank_ref, f32[12,64,24,128]{3,2,1,0:T(8,128)} %bitcast.8, f32[12,64,24,128]{3,2,1,0:T(8,128)} %bitcast.10), custom_call_target="tpu_custom_call" | custom-call | bytes 12000000 | tf_op jit(solution)/shard_map/pack/pallas_call | solution.py:150
  5.4 10.3 %all-to-all-start = ((f32[128,72,128]{2,1,0:T(8,128)}), f32[128,72,128]{2,1,0:T(8,128)}, u32[]{:S(2)}, u32[]{:S(2)}) async-start(f32[128,72,128]{2,1,0:T(8,128)} %pack.1), calls=%async_computation | async-start | bytes 9437184 | tf_op jit(solution)/shard_map/all_to_all | solution.py:367
  15.7 9.9 %local.1 = (bf16[20,256,2304]{2,1,0:T(8,128)(2,1)}, f32[320,128,128]{2,1,0:T(8,128)}) custom-call(s32[1]{0:T(128)} %bitcast.rank_ref, f32[12,1536,128]{2,1,0:T(8,128)} %bitcast.9, f32[12,1536,128]{2,1,0:T(8,128)} %bitcast.11), custom_call_target="tpu_custom_call" | custom-call | flops 20000000000 | bytes 30000000 | tf_op jit(solution)/shard_map/local/pallas_call | solution.py:234
  25.6 47.9 %all-to-all-done.received_ref = f32[128,72,128]{2,1,0:T(8,128)} async-done(((f32[128,72,128]{2,1,0:T(8,128)}), f32[128,72,128]{2,1,0:T(8,128)}, u32[]{:S(2)}, u32[]{:S(2)}) %all-to-all-start) | async-done | bytes 4718624 | tf_op jit(solution)/shard_map/all_to_all | solution.py:367
  73.5 4.5 %mirror.1 = (f32[8,8,128]{2,1,0:T(8,128)S(1)}, f32[8,8,128]{2,1,0:T(8,128)S(1)}) custom-call(s32[1]{0:T(128)} %bitcast.rank_ref, bf16[20,256,2304]{2,1,0:T(8,128)(2,1)} %get-tuple-element.9.left_ref, f32[128,72,128]{2,1,0:T(8,128)} %all-to-all-done.received_ref, f32[320,128,128]{2,1,0:T(8,128)} %get-tuple-element.10.direct_ref), custom_call_target="tpu_custom_call" | custom-call | flops 2500000000 | bytes 10000000 | tf_op jit(solution)/shard_map/mirror/pallas_call | solution.py:337
  78.0 0.1 collective-permute-start
  78.1 1.2 %collective-permute-done = f32[8,8,128]{2,1,0:T(8,128)S(1)} collective-permute-done((f32[8,8,128]{2,1,0:T(8,128)S(1)}, f32[8,8,128]{2,1,0:T(8,128)S(1)}, u32[]{:S(2)}, u32[]{:S(2)}) %collective-permute-start) | collective-permute-done | bytes 32800 | tf_op jit(solution)/shard_map/ppermute | solution.py:370
  79.3 16.6 %all_to_all.10 = f32[64,8,128]{2,1,0:T(8,128)S(1)} all-to-all(f32[64,8,128]{2,1,0:T(8,128)S(1)} %bitcast.12), channel_id=1, replica_groups=mesh['half'=8,'core'=2,'col'=8] {'half','col'}, dimensions={0} | all-to-all | bytes 524288 | tf_op jit(solution)/shard_map/all_to_all | solution.py:373
  96.0 0.7 reduce_sum.9
  (2 shorter events, 0.0 us)
Async XLA Ops:
  5.4 68.1 %all-to-all-start = ((f32[128,72,128]{2,1,0:T(8,128)}), f32[128,72,128]{2,1,0:T(8,128)}, u32[]{:S(2)}, u32[]{:S(2)}) async-start(f32[128,72,128]{2,1,0:T(8,128)} %pack.1), calls=%async_computation | async-start | bytes 9437184 | tf_op jit(solution)/shard_map/all_to_all | solution.py:367
  78.0 1.3 %collective-permute-start = (f32[8,8,128]{2,1,0:T(8,128)S(1)}, f32[8,8,128]{2,1,0:T(8,128)S(1)}, u32[]{:S(2)}, u32[]{:S(2)}) collective-permute-start(f32[8,8,128]{2,1,0:T(8,128)S(1)} %get-tuple-element.12), channel_id=1, source_target_pairs={{0,8},{8,0},{1,9},{9,1},{2,10},{10,2},{3,11},{11,3},{4,12},{12,4},... | collective-permute-start | bytes 98312 | tf_op jit(solution)/shard_map/ppermute | solution.py:370

commit v9 on v8

--- a/solution.py
+++ b/solution.py
@@ -13,7 +13,7 @@
 HALF = WIDTH // 2
 BLOCK = WIDTH * HALF
 LANES = 128
-PACK_PEERS = 16
+PACK_PEERS = 32
 PACK_GROUPS = DEVICES // PACK_PEERS
 PACK_PAIRS = PACK_PEERS // 2
 PAIR_ROWS = 2 * WIDTH

time: 96.9 us -> 97.3 us (level)
  starting transfers between devices: 10.4 us -> 11.7 us
    all_to_all x1, starting transfers between devices: 10.3 us -> 11.6 us  [body(): received = lax.all_to_all(pack(rank, x, v), AXES, 0, 0, tiled=True)]
where the time goes in v9:
time: 97.3 us; the launch traced here: 97.1 us
  waiting for transfers between devices  49.1 us (50%)
  Pallas kernels  18.9 us (19%)
  blocking collectives  16.6 us (17%)
  starting transfers between devices  11.7 us (12%)
    all_to_all x1, waiting for transfers between devices, body(): received = lax.all_to_all(pack(rank, x, v), AXES, 0, 0, tiled=True)  47.9 us
    all_to_all x1, blocking collectives, body(): return jnp.sum(lax.all_to_all(parts, CHIPS, 0, 0, tiled=True), axis=0)  16.6 us
    all_to_all x1, starting transfers between devices, body(): received = lax.all_to_all(pack(rank, x, v), AXES, 0, 0, tiled=True)  11.6 us
    pallas_call x1, Pallas kernels, local(): pl.pallas_call(local_kernel, grid_spec=pltpu.PrefetchScalarGridSpec(num_s...  9.91 us
    pallas_call x1, Pallas kernels, pack(): pl.pallas_call(pack_kernel, in_specs=[pl.BlockSpec(memory_space=pltpu.SME...  4.55 us
    pallas_call x1, Pallas kernels, mirror(): pl.pallas_call(mirror_kernel, in_specs=[pl.BlockSpec(memory_space=pltpu.S...  4.47 us
  transfers between devices with their start and end apart: 2, of which 2 were waited for; matrix products, arithmetic and copies ran while one was open for 0% of the time, Pallas kernels for 10%

profile of v9, /device:TPU:0, one launch (start us, length us, event | category | flops | bytes accessed | tf_op | source)
XLA Modules:
  0.0 97.1 jit_solution(10610762787562304355)
XLA Ops:
  0.0 4.6 %pack.1 = f32[128,72,128]{2,1,0:T(8,128)} custom-call(s32[1]{0:T(128)} %bitcast.rank_ref, f32[12,64,24,128]{3,2,1,0:T(8,128)} %bitcast.8, f32[12,64,24,128]{3,2,1,0:T(8,128)} %bitcast.10), custom_call_target="tpu_custom_call" | custom-call | bytes 12000000 | tf_op jit(solution)/shard_map/pack/pallas_call | solution.py:150
  4.6 11.6 %all-to-all-start = ((f32[128,72,128]{2,1,0:T(8,128)}), f32[128,72,128]{2,1,0:T(8,128)}, u32[]{:S(2)}, u32[]{:S(2)}) async-start(f32[128,72,128]{2,1,0:T(8,128)} %pack.1), calls=%async_computation | async-start | bytes 9437184 | tf_op jit(solution)/shard_map/all_to_all | solution.py:367
  16.1 9.9 %local.1 = (bf16[20,256,2304]{2,1,0:T(8,128)(2,1)}, f32[320,128,128]{2,1,0:T(8,128)}) custom-call(s32[1]{0:T(128)} %bitcast.rank_ref, f32[12,1536,128]{2,1,0:T(8,128)} %bitcast.9, f32[12,1536,128]{2,1,0:T(8,128)} %bitcast.11), custom_call_target="tpu_custom_call" | custom-call | flops 20000000000 | bytes 30000000 | tf_op jit(solution)/shard_map/local/pallas_call | solution.py:234
  26.1 47.9 %all-to-all-done.received_ref = f32[128,72,128]{2,1,0:T(8,128)} async-done(((f32[128,72,128]{2,1,0:T(8,128)}), f32[128,72,128]{2,1,0:T(8,128)}, u32[]{:S(2)}, u32[]{:S(2)}) %all-to-all-start) | async-done | bytes 4718624 | tf_op jit(solution)/shard_map/all_to_all | solution.py:367
  74.0 4.5 %mirror.1 = (f32[8,8,128]{2,1,0:T(8,128)S(1)}, f32[8,8,128]{2,1,0:T(8,128)S(1)}) custom-call(s32[1]{0:T(128)} %bitcast.rank_ref, bf16[20,256,2304]{2,1,0:T(8,128)(2,1)} %get-tuple-element.9.left_ref, f32[128,72,128]{2,1,0:T(8,128)} %all-to-all-done.received_ref, f32[320,128,128]{2,1,0:T(8,128)} %get-tuple-element.10.direct_ref), custom_call_target="tpu_custom_call" | custom-call | flops 2500000000 | bytes 10000000 | tf_op jit(solution)/shard_map/mirror/pallas_call | solution.py:337
  78.5 0.1 collective-permute-start
  78.6 1.2 %collective-permute-done = f32[8,8,128]{2,1,0:T(8,128)S(1)} collective-permute-done((f32[8,8,128]{2,1,0:T(8,128)S(1)}, f32[8,8,128]{2,1,0:T(8,128)S(1)}, u32[]{:S(2)}, u32[]{:S(2)}) %collective-permute-start) | collective-permute-done | bytes 32800 | tf_op jit(solution)/shard_map/ppermute | solution.py:370
  79.8 16.6 %all_to_all.10 = f32[64,8,128]{2,1,0:T(8,128)S(1)} all-to-all(f32[64,8,128]{2,1,0:T(8,128)S(1)} %bitcast.12), channel_id=1, replica_groups=mesh['half'=8,'core'=2,'col'=8] {'half','col'}, dimensions={0} | all-to-all | bytes 524288 | tf_op jit(solution)/shard_map/all_to_all | solution.py:373
  96.4 0.7 reduce_sum.9
  (2 shorter events, 0.0 us)
Async XLA Ops:
  4.6 69.4 %all-to-all-start = ((f32[128,72,128]{2,1,0:T(8,128)}), f32[128,72,128]{2,1,0:T(8,128)}, u32[]{:S(2)}, u32[]{:S(2)}) async-start(f32[128,72,128]{2,1,0:T(8,128)} %pack.1), calls=%async_computation | async-start | bytes 9437184 | tf_op jit(solution)/shard_map/all_to_all | solution.py:367
  78.5 1.3 %collective-permute-start = (f32[8,8,128]{2,1,0:T(8,128)S(1)}, f32[8,8,128]{2,1,0:T(8,128)S(1)}, u32[]{:S(2)}, u32[]{:S(2)}) collective-permute-start(f32[8,8,128]{2,1,0:T(8,128)S(1)} %get-tuple-element.12), channel_id=1, source_target_pairs={{0,8},{8,0},{1,9},{9,1},{2,10},{10,2},{3,11},{11,3},{4,12},{12,4},... | collective-permute-start | bytes 98312 | tf_op jit(solution)/shard_map/ppermute | solution.py:370
